TPU v7x, 32 devices: a whole 2x2x4 slice. The times are simulated.
32 devices in a mesh: dp: 4 (over x, core), fsdp: 8 (over z, y).
Axes of the slice: x: 2, y: 2, z: 4, core: 2. Of those that a mesh axis runs over, the one named last changes fastest.
Arguments:
- inputs: bfloat16 [16384, 768], P(('dp', 'fsdp')), may hold values from -6 to 6
- cotangent: bfloat16 [16384, 768], P(('dp', 'fsdp')), may hold values from -6 to 6
- lengths: int32 [128], P(('dp', 'fsdp')), may hold values from 96 to 128, as said below
- tags: int32 [128, 1], P(('dp', 'fsdp')), may hold values from 0 to 1; in each aligned block of 4 rows (0 to 3, 4 to 7, ...) at most 3 rows name the same one
- query_weight: bfloat16 [2, 768, 768], P(None, ('dp', 'fsdp')), may hold values from -0.21875 to 0.21875
- query_bias: bfloat16 [2, 768], P(None, ('dp', 'fsdp')), may hold values from -3 to 3
- key_weight: bfloat16 [2, 768, 768], P(None, ('dp', 'fsdp')), may hold values from -0.21875 to 0.21875
- value_weight: bfloat16 [2, 768, 768], P(None, ('dp', 'fsdp')), may hold values from -0.21875 to 0.21875
- value_bias: bfloat16 [2, 768], P(None, ('dp', 'fsdp')), may hold values from -1.75 to 1.75
- output_projection_weight: bfloat16 [2, 768, 768], P(None, ('dp', 'fsdp')), may hold values from -0.875 to 0.875
- out_bias: bfloat16 [2, 768], P(None, ('dp', 'fsdp')), may hold values from -1.75 to 1.75
- first_gain: bfloat16 [2, 768], P(None, ('dp', 'fsdp')), may hold values from 0.099609375 to 1.8984375
- first_shift: bfloat16 [2, 768], P(None, ('dp', 'fsdp')), may hold values from -1.75 to 1.75
- up_weight: bfloat16 [2, 768, 3072], P(None, ('dp', 'fsdp')), may hold values from -0.21875 to 0.21875
- up_bias: bfloat16 [2, 3072], P(None, ('dp', 'fsdp')), may hold values from -1.75 to 1.75
- down_weight: bfloat16 [2, 3072, 768], P(None, ('dp', 'fsdp')), may hold values from -0.109375 to 0.109375
- down_bias: bfloat16 [2, 768], P(None, ('dp', 'fsdp')), may hold values from -1.75 to 1.75
- second_gain: bfloat16 [2, 768], P(None, ('dp', 'fsdp')), may hold values from 0.099609375 to 1.8984375
- second_shift: bfloat16 [2, 768], P(None, ('dp', 'fsdp')), may hold values from -1.75 to 1.75
Outputs:
- output: bfloat16 [16384, 768], P(('dp', 'fsdp'))
- input_grad: bfloat16 [16384, 768], P(('dp', 'fsdp'))
- grad_query_weight: float32 [2, 768, 768], P(None, ('dp', 'fsdp'))
- grad_query_bias: float32 [2, 768], P(None, ('dp', 'fsdp'))
- grad_key_weight: float32 [2, 768, 768], P(None, ('dp', 'fsdp'))
- grad_value_weight: float32 [2, 768, 768], P(None, ('dp', 'fsdp'))
- grad_value_bias: float32 [2, 768], P(None, ('dp', 'fsdp'))
- grad_out_weight: float32 [2, 768, 768], P(None, ('dp', 'fsdp'))
- grad_out_bias: float32 [2, 768], P(None, ('dp', 'fsdp'))
- grad_first_gain: float32 [2, 768], P(None, ('dp', 'fsdp'))
- grad_first_shift: float32 [2, 768], P(None, ('dp', 'fsdp'))
- grad_up_weight: float32 [2, 768, 3072], P(None, ('dp', 'fsdp'))
- grad_up_bias: float32 [2, 3072], P(None, ('dp', 'fsdp'))
- grad_down_weight: float32 [2, 3072, 768], P(None, ('dp', 'fsdp'))
- grad_down_bias: float32 [2, 768], P(None, ('dp', 'fsdp'))
- grad_second_gain: float32 [2, 768], P(None, ('dp', 'fsdp'))
- grad_second_shift: float32 [2, 768], P(None, ('dp', 'fsdp'))
Inputs may be any that keep to these rules, and one draw needn't show every extreme that they name: `lengths`: some chain has exactly 128 live slots and some exactly 96. `tags`: among the 4 chains of one device at most 3 carry either tag, and some device holds exactly 3 of one tag.
All inputs are finite; a program needn't handle non-finite values.
Results may differ from a plain program's by a relative error of at most 0.02.
Values may be sent and summed in bfloat16 or wider, within the bound.
No kernel may reach another device: no remote copies, remote signals or barrier semaphores. Data moves between devices by JAX's collectives and lax.ppermute only.
A program may use at most 192 MiB of HBM per device.

v0:
```python
import jax
import jax.numpy as jnp
from jax import lax
from jax.sharding import PartitionSpec as P

HEADS = 12
HEAD_DIM = 64
CAP = 3


def matmul(left_side, right_side):
    return jnp.dot(left_side, right_side, preferred_element_type=jnp.float32)


def matmul_t(left_side, right_side):
    return lax.dot_general(
        left_side, right_side, (((0,), (0,)), ((), ())), preferred_element_type=jnp.float32
    )


def matmul_nt(left_side, right_side):
    return lax.dot_general(
        left_side, right_side, (((1,), (1,)), ((), ())), preferred_element_type=jnp.float32
    )


def layer_norm(values, norm_gain, norm_shift):
    centre = values - jnp.mean(values, axis=-1, keepdims=True)
    return (
        centre * lax.rsqrt(jnp.mean(centre * centre, axis=-1, keepdims=True) + 1e-05) * norm_gain
        + norm_shift
    )


def exact_gelu(hidden):
    return jax.nn.gelu(hidden, approximate=False)


def selector(tags, model_index):
    member = (tags[:, 0] == model_index).astype(jnp.int32)
    ranking = jnp.cumsum(member) - 1
    places = lax.broadcasted_iota(jnp.int32, (CAP, member.shape[0]), 0)
    return (places == ranking[None, :]) & (member[None, :] == 1)


def attention_scores(queries, key_rows, slot_len):
    scores = jnp.einsum(
        "sqhe,skhe->shqk", queries, key_rows, preferred_element_type=jnp.float32
    ) * HEAD_DIM ** (-0.5)
    positions = lax.broadcasted_iota(jnp.int32, (1, 1, 1, key_rows.shape[1]), 3)
    return jnp.where(positions < slot_len[:, None, None, None], scores, -1000000000.0)


def forward(slot_block, slot_len, params):
    (
        query_weight,
        query_bias,
        key_weight,
        value_weight,
        value_bias,
        output_projection_weight,
        out_bias,
        first_gain,
        first_shift,
        up_weight,
        up_bias,
        down_weight,
        down_bias,
        second_gain,
        second_shift,
    ) = params
    slots, slot_length, model_width = slot_block.shape
    head_shape = (slots, slot_length, HEADS, HEAD_DIM)
    flat_rows = slot_block.reshape(slots * slot_length, model_width)
    queries = (
        (matmul(flat_rows, query_weight) + query_bias).astype(jnp.bfloat16).reshape(head_shape)
    )
    key_rows = matmul(flat_rows, key_weight).astype(jnp.bfloat16).reshape(head_shape)
    value_rows = (
        (matmul(flat_rows, value_weight) + value_bias).astype(jnp.bfloat16).reshape(head_shape)
    )
    scores = attention_scores(queries, key_rows, slot_len)
    row_top = jnp.max(scores, axis=-1, keepdims=True)
    row_total = jnp.sum(jnp.exp(scores - row_top), axis=-1, keepdims=True)
    logarithm_total = row_top + jnp.log(row_total)
    probs_low = jnp.exp(scores - logarithm_total).astype(jnp.bfloat16)
    context = jnp.einsum(
        "shqk,skhe->sqhe", probs_low, value_rows, preferred_element_type=jnp.float32
    )
    context = context.reshape(slots * slot_length, model_width).astype(jnp.bfloat16)
    first_in = flat_rows.astype(jnp.float32) + matmul(context, output_projection_weight) + out_bias
    normed_first = layer_norm(first_in, first_gain, first_shift)
    first_low = normed_first.astype(jnp.bfloat16)
    hidden = matmul(first_low, up_weight) + up_bias
    active = exact_gelu(hidden).astype(jnp.bfloat16)
    second_in = normed_first + matmul(active, down_weight) + down_bias
    result = layer_norm(second_in, second_gain, second_shift)
    stored = (
        flat_rows,
        queries,
        key_rows,
        value_rows,
        logarithm_total,
        context,
        first_in,
        first_low,
        hidden,
        active,
        second_in,
    )
    return (result, stored)


def backward(grad_out, slot_len, params, stored):
    (
        query_weight,
        query_bias,
        key_weight,
        value_weight,
        value_bias,
        output_projection_weight,
        out_bias,
        first_gain,
        first_shift,
        up_weight,
        up_bias,
        down_weight,
        down_bias,
        second_gain,
        second_shift,
    ) = params
    (
        flat_rows,
        queries,
        key_rows,
        value_rows,
        logarithm_total,
        context,
        first_in,
        first_low,
        hidden,
        active,
        second_in,
    ) = stored
    row_count, model_width = flat_rows.shape
    head_shape = queries.shape
    _, second_back = jax.vjp(
        layer_norm, second_in, second_gain.astype(jnp.float32), second_shift.astype(jnp.float32)
    )
    grad_second, grad_second_gain, grad_second_shift = second_back(grad_out)
    down_grad = grad_second.astype(jnp.bfloat16)
    grad_down_bias = jnp.sum(down_grad.astype(jnp.float32), axis=0)
    grad_down_weight = matmul_t(active, down_grad)
    _, gelu_back = jax.vjp(exact_gelu, hidden)
    up_grad = gelu_back(matmul_nt(down_grad, down_weight))[0].astype(jnp.bfloat16)
    grad_up_bias = jnp.sum(up_grad.astype(jnp.float32), axis=0)
    grad_up_weight = matmul_t(first_low, up_grad)
    first_grad = grad_second + matmul_nt(up_grad, up_weight)
    _, first_back = jax.vjp(
        layer_norm, first_in, first_gain.astype(jnp.float32), first_shift.astype(jnp.float32)
    )
    grad_first_in, grad_first_gain, grad_first_shift = first_back(first_grad)
    branch_grad = grad_first_in.astype(jnp.bfloat16)
    grad_out_bias = jnp.sum(branch_grad.astype(jnp.float32), axis=0)
    grad_out_weight = matmul_t(context, branch_grad)
    context_grad = (
        matmul_nt(branch_grad, output_projection_weight).astype(jnp.bfloat16).reshape(head_shape)
    )
    scores = attention_scores(queries, key_rows, slot_len)
    probs = jnp.exp(scores - logarithm_total)
    probs_low = probs.astype(jnp.bfloat16)
    value_grad = jnp.einsum(
        "shqk,sqhe->skhe", probs_low, context_grad, preferred_element_type=jnp.float32
    )
    value_grad = value_grad.astype(jnp.bfloat16).reshape(row_count, model_width)
    probs_grad = jnp.einsum(
        "sqhe,skhe->shqk", context_grad, value_rows, preferred_element_type=jnp.float32
    )
    score_grad = (
        probs * (probs_grad - jnp.sum(probs_grad * probs, axis=-1, keepdims=True))
    ).astype(jnp.bfloat16)
    scaling = HEAD_DIM ** (-0.5)
    query_grad = scaling * jnp.einsum(
        "shqk,skhe->sqhe", score_grad, key_rows, preferred_element_type=jnp.float32
    )
    query_grad = query_grad.astype(jnp.bfloat16).reshape(row_count, model_width)
    key_grad = scaling * jnp.einsum(
        "shqk,sqhe->skhe", score_grad, queries, preferred_element_type=jnp.float32
    )
    key_grad = key_grad.astype(jnp.bfloat16).reshape(row_count, model_width)
    grad_query_bias = jnp.sum(query_grad.astype(jnp.float32), axis=0)
    grad_value_bias = jnp.sum(value_grad.astype(jnp.float32), axis=0)
    grad_query_weight = matmul_t(flat_rows, query_grad)
    grad_key_weight = matmul_t(flat_rows, key_grad)
    grad_value_weight = matmul_t(flat_rows, value_grad)
    rows_grad = (
        grad_first_in
        + matmul_nt(query_grad, query_weight)
        + matmul_nt(key_grad, key_weight)
        + matmul_nt(value_grad, value_weight)
    )
    gradients = (
        grad_query_weight,
        grad_query_bias,
        grad_key_weight,
        grad_value_weight,
        grad_value_bias,
        grad_out_weight,
        grad_out_bias,
        grad_first_gain,
        grad_first_shift,
        grad_up_weight,
        grad_up_bias,
        grad_down_weight,
        grad_down_bias,
        grad_second_gain,
        grad_second_shift,
    )
    return (rows_grad, gradients)


def reduce_both(incoming_gradients):
    dp_count = lax.axis_size("dp")
    fsdp_count = lax.axis_size("fsdp")
    split = tuple(
        (
            grad.reshape(
                (2, dp_count, fsdp_count, grad.shape[1] // (dp_count * fsdp_count)) + grad.shape[2:]
            )
            for grad in incoming_gradients
        )
    )
    column = (
        lax.psum_scatter(
            split[0].astype(jnp.bfloat16), "fsdp", scatter_dimension=2, tiled=True
        ).astype(jnp.float32),
        lax.psum_scatter(
            split[1].astype(jnp.bfloat16), "fsdp", scatter_dimension=2, tiled=True
        ).astype(jnp.float32),
        lax.psum_scatter(
            split[2].astype(jnp.bfloat16), "fsdp", scatter_dimension=2, tiled=True
        ).astype(jnp.float32),
        lax.psum_scatter(
            split[3].astype(jnp.bfloat16), "fsdp", scatter_dimension=2, tiled=True
        ).astype(jnp.float32),
        lax.psum_scatter(
            split[4].astype(jnp.bfloat16), "fsdp", scatter_dimension=2, tiled=True
        ).astype(jnp.float32),
        lax.psum_scatter(
            split[5].astype(jnp.bfloat16), "fsdp", scatter_dimension=2, tiled=True
        ).astype(jnp.float32),
        lax.psum_scatter(
            split[6].astype(jnp.bfloat16), "fsdp", scatter_dimension=2, tiled=True
        ).astype(jnp.float32),
        lax.psum_scatter(
            split[7].astype(jnp.bfloat16), "fsdp", scatter_dimension=2, tiled=True
        ).astype(jnp.float32),
        lax.psum_scatter(
            split[8].astype(jnp.bfloat16), "fsdp", scatter_dimension=2, tiled=True
        ).astype(jnp.float32),
        lax.psum_scatter(
            split[9].astype(jnp.bfloat16), "fsdp", scatter_dimension=2, tiled=True
        ).astype(jnp.float32),
        lax.psum_scatter(
            split[10].astype(jnp.bfloat16), "fsdp", scatter_dimension=2, tiled=True
        ).astype(jnp.float32),
        lax.psum_scatter(
            split[11].astype(jnp.bfloat16), "fsdp", scatter_dimension=2, tiled=True
        ).astype(jnp.float32),
        lax.psum_scatter(
            split[12].astype(jnp.bfloat16), "fsdp", scatter_dimension=2, tiled=True
        ).astype(jnp.float32),
        lax.psum_scatter(
            split[13].astype(jnp.bfloat16), "fsdp", scatter_dimension=2, tiled=True
        ).astype(jnp.float32),
        lax.psum_scatter(
            split[14].astype(jnp.bfloat16), "fsdp", scatter_dimension=2, tiled=True
        ).astype(jnp.float32),
    )
    owned = (
        lax.psum_scatter(
            column[0].astype(jnp.bfloat16), "dp", scatter_dimension=1, tiled=True
        ).astype(jnp.float32),
        lax.psum_scatter(
            column[1].astype(jnp.bfloat16), "dp", scatter_dimension=1, tiled=True
        ).astype(jnp.float32),
        lax.psum_scatter(
            column[2].astype(jnp.bfloat16), "dp", scatter_dimension=1, tiled=True
        ).astype(jnp.float32),
        lax.psum_scatter(
            column[3].astype(jnp.bfloat16), "dp", scatter_dimension=1, tiled=True
        ).astype(jnp.float32),
        lax.psum_scatter(
            column[4].astype(jnp.bfloat16), "dp", scatter_dimension=1, tiled=True
        ).astype(jnp.float32),
        lax.psum_scatter(
            column[5].astype(jnp.bfloat16), "dp", scatter_dimension=1, tiled=True
        ).astype(jnp.float32),
        lax.psum_scatter(
            column[6].astype(jnp.bfloat16), "dp", scatter_dimension=1, tiled=True
        ).astype(jnp.float32),
        lax.psum_scatter(
            column[7].astype(jnp.bfloat16), "dp", scatter_dimension=1, tiled=True
        ).astype(jnp.float32),
        lax.psum_scatter(
            column[8].astype(jnp.bfloat16), "dp", scatter_dimension=1, tiled=True
        ).astype(jnp.float32),
        lax.psum_scatter(
            column[9].astype(jnp.bfloat16), "dp", scatter_dimension=1, tiled=True
        ).astype(jnp.float32),
        lax.psum_scatter(
            column[10].astype(jnp.bfloat16), "dp", scatter_dimension=1, tiled=True
        ).astype(jnp.float32),
        lax.psum_scatter(
            column[11].astype(jnp.bfloat16), "dp", scatter_dimension=1, tiled=True
        ).astype(jnp.float32),
        lax.psum_scatter(
            column[12].astype(jnp.bfloat16), "dp", scatter_dimension=1, tiled=True
        ).astype(jnp.float32),
        lax.psum_scatter(
            column[13].astype(jnp.bfloat16), "dp", scatter_dimension=1, tiled=True
        ).astype(jnp.float32),
        lax.psum_scatter(
            column[14].astype(jnp.bfloat16), "dp", scatter_dimension=1, tiled=True
        ).astype(jnp.float32),
    )
    return tuple((piece.reshape((2,) + piece.shape[3:]) for piece in owned))


def mixed_body(
    inputs,
    cotangent,
    lengths,
    tags,
    query_weight,
    query_bias,
    key_weight,
    value_weight,
    value_bias,
    output_projection_weight,
    out_bias,
    first_gain,
    first_shift,
    up_weight,
    up_bias,
    down_weight,
    down_bias,
    second_gain,
    second_shift,
):
    gathered = (
        lax.all_gather(query_weight, ("dp", "fsdp"), axis=1, tiled=True),
        lax.all_gather(query_bias, ("dp", "fsdp"), axis=1, tiled=True),
        lax.all_gather(key_weight, ("dp", "fsdp"), axis=1, tiled=True),
        lax.all_gather(value_weight, ("dp", "fsdp"), axis=1, tiled=True),
        lax.all_gather(value_bias, ("dp", "fsdp"), axis=1, tiled=True),
        lax.all_gather(output_projection_weight, ("dp", "fsdp"), axis=1, tiled=True),
        lax.all_gather(out_bias, ("dp", "fsdp"), axis=1, tiled=True),
        lax.all_gather(first_gain, ("dp", "fsdp"), axis=1, tiled=True),
        lax.all_gather(first_shift, ("dp", "fsdp"), axis=1, tiled=True),
        lax.all_gather(up_weight, ("dp", "fsdp"), axis=1, tiled=True),
        lax.all_gather(up_bias, ("dp", "fsdp"), axis=1, tiled=True),
        lax.all_gather(down_weight, ("dp", "fsdp"), axis=1, tiled=True),
        lax.all_gather(down_bias, ("dp", "fsdp"), axis=1, tiled=True),
        lax.all_gather(second_gain, ("dp", "fsdp"), axis=1, tiled=True),
        lax.all_gather(second_shift, ("dp", "fsdp"), axis=1, tiled=True),
    )
    chain_count = lengths.shape[0]
    model_width = inputs.shape[1]
    slot_length = inputs.shape[0] // chain_count
    chain_token_rows = inputs.reshape(chain_count, slot_length, model_width)
    chain_gradient_rows = cotangent.reshape(chain_count, slot_length, model_width)
    output = jnp.zeros((chain_count, slot_length, model_width), jnp.float32)
    saved = []
    for model_index in range(2):
        chosen = selector(tags, model_index)
        selected_lower_precision = chosen.astype(jnp.bfloat16)
        chosen_full = chosen.astype(jnp.float32)
        slot_len = jnp.sum(jnp.where(chosen, lengths[None, :], 0), axis=1)
        slot_block = jnp.einsum(
            "sn,ngl->sgl",
            selected_lower_precision,
            chain_token_rows,
            preferred_element_type=jnp.float32,
        )
        result, stored = forward(
            slot_block.astype(jnp.bfloat16),
            slot_len,
            tuple((tensor[model_index] for tensor in gathered)),
        )
        output = output + jnp.einsum(
            "nm,nka->mka",
            chosen_full,
            result.reshape(CAP, slot_length, model_width),
            precision=lax.Precision.HIGHEST,
        )
        saved.append((selected_lower_precision, chosen_full, slot_len, stored))
    gathered = (
        lax.all_gather(query_weight, ("dp", "fsdp"), axis=1, tiled=True),
        lax.all_gather(query_bias, ("dp", "fsdp"), axis=1, tiled=True),
        lax.all_gather(key_weight, ("dp", "fsdp"), axis=1, tiled=True),
        lax.all_gather(value_weight, ("dp", "fsdp"), axis=1, tiled=True),
        lax.all_gather(value_bias, ("dp", "fsdp"), axis=1, tiled=True),
        lax.all_gather(output_projection_weight, ("dp", "fsdp"), axis=1, tiled=True),
        lax.all_gather(out_bias, ("dp", "fsdp"), axis=1, tiled=True),
        lax.all_gather(first_gain, ("dp", "fsdp"), axis=1, tiled=True),
        lax.all_gather(first_shift, ("dp", "fsdp"), axis=1, tiled=True),
        lax.all_gather(up_weight, ("dp", "fsdp"), axis=1, tiled=True),
        lax.all_gather(up_bias, ("dp", "fsdp"), axis=1, tiled=True),
        lax.all_gather(down_weight, ("dp", "fsdp"), axis=1, tiled=True),
        lax.all_gather(down_bias, ("dp", "fsdp"), axis=1, tiled=True),
        lax.all_gather(second_gain, ("dp", "fsdp"), axis=1, tiled=True),
        lax.all_gather(second_shift, ("dp", "fsdp"), axis=1, tiled=True),
    )
    input_grad = jnp.zeros((chain_count, slot_length, model_width), jnp.float32)
    model_grads = []
    for model_index in range(2):
        selected_lower_precision, chosen_full, slot_len, stored = saved[model_index]
        grad_block = jnp.einsum(
            "sn,ngl->sgl",
            selected_lower_precision,
            chain_gradient_rows,
            preferred_element_type=jnp.float32,
        )
        rows_grad, gradients = backward(
            grad_block.reshape(CAP * slot_length, model_width),
            slot_len,
            tuple((tensor[model_index] for tensor in gathered)),
            stored,
        )
        input_grad = input_grad + jnp.einsum(
            "nm,nka->mka",
            chosen_full,
            rows_grad.reshape(CAP, slot_length, model_width),
            precision=lax.Precision.HIGHEST,
        )
        model_grads.append(gradients)
    stacked = tuple(
        (
            jnp.stack([heavy_part, light_part])
            for heavy_part, light_part in zip(model_grads[0], model_grads[1])
        )
    )
    reduced = reduce_both(stacked)
    return (
        output.reshape(chain_count * slot_length, model_width).astype(jnp.bfloat16),
        input_grad.reshape(chain_count * slot_length, model_width).astype(jnp.bfloat16),
    ) + tuple(reduced)


def on_device(
    inputs,
    cotangent,
    lengths,
    tags,
    query_weight,
    query_bias,
    key_weight,
    value_weight,
    value_bias,
    output_projection_weight,
    out_bias,
    first_gain,
    first_shift,
    up_weight,
    up_bias,
    down_weight,
    down_bias,
    second_gain,
    second_shift,
):
    return mixed_body(
        inputs,
        cotangent,
        lengths,
        tags,
        query_weight,
        query_bias,
        key_weight,
        value_weight,
        value_bias,
        output_projection_weight,
        out_bias,
        first_gain,
        first_shift,
        up_weight,
        up_bias,
        down_weight,
        down_bias,
        second_gain,
        second_shift,
    )


def solution(mesh):
    placed = (
        P(("dp", "fsdp"), None),
        P(("dp", "fsdp"), None),
        P(("dp", "fsdp")),
        P(("dp", "fsdp"), None),
        P(None, ("dp", "fsdp"), None),
        P(None, ("dp", "fsdp")),
        P(None, ("dp", "fsdp"), None),
        P(None, ("dp", "fsdp"), None),
        P(None, ("dp", "fsdp")),
        P(None, ("dp", "fsdp"), None),
        P(None, ("dp", "fsdp")),
        P(None, ("dp", "fsdp")),
        P(None, ("dp", "fsdp")),
        P(None, ("dp", "fsdp"), None),
        P(None, ("dp", "fsdp")),
        P(None, ("dp", "fsdp"), None),
        P(None, ("dp", "fsdp")),
        P(None, ("dp", "fsdp")),
        P(None, ("dp", "fsdp")),
    )
    return jax.shard_map(
        on_device,
        mesh=mesh,
        in_specs=placed,
        out_specs=(
            P(("dp", "fsdp"), None),
            P(("dp", "fsdp"), None),
            P(None, ("dp", "fsdp"), None),
            P(None, ("dp", "fsdp")),
            P(None, ("dp", "fsdp"), None),
            P(None, ("dp", "fsdp"), None),
            P(None, ("dp", "fsdp")),
            P(None, ("dp", "fsdp"), None),
            P(None, ("dp", "fsdp")),
            P(None, ("dp", "fsdp")),
            P(None, ("dp", "fsdp")),
            P(None, ("dp", "fsdp"), None),
            P(None, ("dp", "fsdp")),
            P(None, ("dp", "fsdp"), None),
            P(None, ("dp", "fsdp")),
            P(None, ("dp", "fsdp")),
            P(None, ("dp", "fsdp")),
        ),
        check_vma=False,
    )
```

profile of v0, /device:TPU:0, one launch (start us, length us, event | category | flops | bytes accessed | tf_op | source)
XLA Modules:
  0.0 1756.8 jit_solution(9716525547677283607)
XLA Ops:
  12.2 69.5 %all-gather.1 = bf16[32,24,2]{1,2,0:T(2,128)(2,1)S(1)} all-gather(bf16[1,24,2]{1,2,0:T(2,128)(2,1)} %bitcast.560), channel_id=1, replica_groups=mesh['dp'=4,'fsdp'=8] {'dp','fsdp'}, dimensions={0}, use_global_device_ids=true | all-gather | bytes 3168 | tf_op jit(solution)/shard_map/all_gather | solution.py:353
  81.8 63.2 %all-gather = bf16[32,24,2]{1,2,0:T(2,128)(2,1)S(1)} all-gather(bf16[1,24,2]{1,2,0:T(2,128)(2,1)} %bitcast.561), channel_id=1, replica_groups=mesh['dp'=4,'fsdp'=8] {'dp','fsdp'}, dimensions={0}, use_global_device_ids=true | all-gather | bytes 3168 | tf_op jit(solution)/shard_map/all_gather | solution.py:356
  145.1 65.4 %all-gather.2 = bf16[32,24,2]{1,2,0:T(2,128)(2,1)S(1)} all-gather(bf16[1,24,2]{1,2,0:T(2,128)(2,1)} %bitcast.562), channel_id=1, replica_groups=mesh['dp'=4,'fsdp'=8] {'dp','fsdp'}, dimensions={0}, use_global_device_ids=true | all-gather | bytes 3168 | tf_op jit(solution)/shard_map/all_gather | solution.py:358
  210.7 63.2 %all-gather.3 = bf16[32,24,2]{1,2,0:T(2,128)(2,1)S(1)} all-gather(bf16[1,24,2]{1,2,0:T(2,128)(2,1)} %bitcast.563), channel_id=1, replica_groups=mesh['dp'=4,'fsdp'=8] {'dp','fsdp'}, dimensions={0}, use_global_device_ids=true | all-gather | bytes 3168 | tf_op jit(solution)/shard_map/all_gather | solution.py:359
  274.0 65.9 %all-gather.4 = bf16[32,24,2]{1,2,0:T(2,128)(2,1)S(1)} all-gather(bf16[1,24,2]{1,2,0:T(2,128)(2,1)} %bitcast.564), channel_id=1, replica_groups=mesh['dp'=4,'fsdp'=8] {'dp','fsdp'}, dimensions={0}, use_global_device_ids=true | all-gather | bytes 3168 | tf_op jit(solution)/shard_map/all_gather | solution.py:360
  340.0 63.5 %all-gather.5 = bf16[32,96,2]{1,2,0:T(2,128)(2,1)S(1)} all-gather(bf16[1,96,2]{1,2,0:T(2,128)(2,1)} %bitcast.565), channel_id=1, replica_groups=mesh['dp'=4,'fsdp'=8] {'dp','fsdp'}, dimensions={0}, use_global_device_ids=true | all-gather | bytes 12672 | tf_op jit(solution)/shard_map/all_gather | solution.py:362
  403.6 65.5 %all-gather.6 = bf16[32,24,2]{1,2,0:T(2,128)(2,1)S(1)} all-gather(bf16[1,24,2]{1,2,0:T(2,128)(2,1)} %bitcast.566), channel_id=1, replica_groups=mesh['dp'=4,'fsdp'=8] {'dp','fsdp'}, dimensions={0}, use_global_device_ids=true | all-gather | bytes 3168 | tf_op jit(solution)/shard_map/all_gather | solution.py:364
  469.1 63.1 %all-gather.7 = bf16[32,24,2]{1,2,0:T(2,128)(2,1)S(1)} all-gather(bf16[1,24,2]{1,2,0:T(2,128)(2,1)} %bitcast.567), channel_id=1, replica_groups=mesh['dp'=4,'fsdp'=8] {'dp','fsdp'}, dimensions={0}, use_global_device_ids=true | all-gather | bytes 3168 | tf_op jit(solution)/shard_map/all_gather | solution.py:365
  532.4 65.3 %all-gather.8 = bf16[32,24,2]{1,2,0:T(2,128)(2,1)S(1)} all-gather(bf16[1,24,2]{1,2,0:T(2,128)(2,1)} %bitcast.568), channel_id=1, replica_groups=mesh['dp'=4,'fsdp'=8] {'dp','fsdp'}, dimensions={0}, use_global_device_ids=true | all-gather | bytes 3168 | tf_op jit(solution)/shard_map/all_gather | solution.py:366
  598.6 2.0 convolution_convert_fusion.13
  609.7 1.9 convolution_convert_fusion.19
  614.5 1.9 fusion.50
  619.1 1.9 fusion.51
  623.7 1.9 convolution_convert_fusion.21
  628.0 1.9 fusion.48
  632.6 1.9 fusion.49
  635.5 1.9 copy.171
  637.4 1.9 fusion.18
  645.9 2.5 fusion.174
  650.8 16.3 multiply_convert_fusion
  667.2 5.6 fusion.173
  675.6 4.3 convolution_convert_fusion
  680.0 7.2 fusion.180
  687.2 4.7 convolution_convert_fusion.2
  691.9 2.4 multiply_reduce_fusion.2
  694.3 13.6 multiply_convert_fusion.1
  707.9 2.1 fusion.175
  712.6 7.2 fusion.181
  719.8 5.0 convolution_convert_fusion.3
  724.9 2.4 multiply_reduce_fusion.3
  732.7 2.8 reshape.805
  735.5 2.6 copy.217
  738.1 3.8 fusion.178
  749.6 2.8 reshape.804
  752.4 2.6 copy.201
  755.0 2.2 fusion.179
  761.2 4.4 convolution_convert_fusion.1
  769.9 1.9 fusion.39
  774.5 1.8 fusion.38
  776.4 1.9 fusion.36
  778.3 1.9 fusion.34
  781.7 8.4 pad_maximum_fusion
  790.1 3.4 pad_maximum_fusion.4
  796.7 8.3 pad_maximum_fusion.1
  807.6 2.1 fusion.24
  809.7 2.4 add_convert_fusion.3
  814.4 39.5 %all-reduce.28 = (bf16[2,4,8,24]{3,1,0,2:T(4,128)(2,1)S(1)}, bf16[2,4,8,24]{3,1,0,2:T(4,128)(2,1)S(1)}, bf16[2,4,8,24]{3,1,0,2:T(4,128)(2,1)S(1)}, bf16[2,4,8,24...) all-reduce(bf16[2,4,8,24]{3,1,0,2:T(4,128)(2,1)S(1)} %copy.234, ...), channel_id=4, replica_groups=mesh['dp'=4,'fsdp'=8] {'fsdp'}, use_global_device_ids=true, to_apply=%region_30.31.clone | all-reduce | flops 18432 | bytes 73728
  862.0 782.6 %all-reduce.35.cloned.1.call-done = (bf16[2,4,8,24,768]{4,3,2,1,0:T(8,128)(2,1)}, bf16[2,4,8,24,768]{4,3,2,1,0:T(8,128)(2,1)}, bf16[2,4,8,24,768]{4,3,2,1,0:T(8,...) async-done(((bf16[2,4,8,24,768]{4,3,2,1,0:T(8,128)(2,1)}, ...) | async-done | bytes 28311568
  1644.6 2.3 constant_dynamic-slice_fusion.23
  1647.0 2.3 constant_dynamic-slice_fusion.20
  1649.3 2.3 constant_dynamic-slice_fusion.19
  1651.6 2.4 constant_dynamic-slice_fusion.16
  1656.7 3.1 constant_dynamic-slice_fusion.9
  1660.2 2.1 convolution_add_fusion.4
  1665.0 2.1 fusion.20
  1670.1 3.0 constant_dynamic-slice_fusion.6
  1673.2 2.3 add_convert_fusion.2
  1676.4 12.4 all-reduce.30
  1699.9 2.2 bitcast_convert_fusion.5
  1702.2 2.2 bitcast_convert_fusion.4
  1704.4 2.2 bitcast_convert_fusion.3
  1706.6 2.2 bitcast_convert_fusion.2
  1708.9 10.8 reduce-scatter.17.cloned.1.call-done
  1721.5 26.3 %reduce-scatter.19.cloned.1.call-done = bf16[2,1,1,96,768]{4,3,0,2,1:T(8,128)(2,1)} async-done(((bf16[2,4,1,96,768]{4,3,0,2,1:T(8,128)(2,1)}), bf16[2,1,1,96,768]{4,3,0,2,1:T(8,128)(2,1)}) %reduce-scatter.19.cloned.1.call-update) | async-done | bytes 294928 | tf_op jit(solution)/shard_map/reduce_scatter | solution.py:314
  (393 shorter events, 109.9 us)
Async XLA Ops:
  7.2 596.5 %copy-start = (bf16[512,768]{1,0:T(8,128)(2,1)S(1)}, bf16[512,768]{1,0:T(8,128)(2,1)}, u32[]{:S(2)}) copy-start(bf16[512,768]{1,0:T(8,128)(2,1)} %param.20) | copy-start | bytes 2359300
  7.2 602.5 %all-gather.20.cloned.1.call-start = ((), (), s32[]{:S(2)}) async-start(), calls=%async_computation.4 | async-start | bytes 2433024 | tf_op jit(solution)/shard_map/all_gather | solution.py:354
  7.9 606.5 %all-gather.16.cloned.1.call-start = ((), (), s32[]{:S(2)}) async-start(), calls=%async_computation.2 | async-start | bytes 2433024 | tf_op jit(solution)/shard_map/all_gather | solution.py:355
  8.7 610.4 %all-gather.18.cloned.1.call-start = ((), (), s32[]{:S(2)}) async-start(), calls=%async_computation.3 | async-start | bytes 2433024 | tf_op jit(solution)/shard_map/all_gather | solution.py:352
  9.4 636.5 %all-gather.22.cloned.1.call-start = ((), (), s32[]{:S(2)}) async-start(), calls=%async_computation.5 | async-start | bytes 2433024 | tf_op jit(solution)/shard_map/all_gather | solution.py:357
  10.0 640.8 %all-gather.24.cloned.1.call-start = ((), (), s32[]{:S(2)}) async-start(), calls=%async_computation.6 | async-start | bytes 9732096 | tf_op jit(solution)/shard_map/all_gather | solution.py:361
  10.6 656.6 %all-gather.26.cloned.1.call-start = ((), (), s32[]{:S(2)}) async-start(), calls=%async_computation.7 | async-start | bytes 9732096 | tf_op jit(solution)/shard_map/all_gather | solution.py:363
  11.2 1633.4 %all-reduce.35.cloned.1.call-start = ((), (), s32[]{:S(2)}) async-start(), calls=%async_computation.10 | async-start | bytes 56623104
  403.5 198.2 %copy-start.71 = (bf16[512,768]{1,0:T(8,128)(2,1)S(1)}, bf16[512,768]{1,0:T(8,128)(2,1)}, u32[]{:S(2)}) copy-start(bf16[512,768]{1,0:T(8,128)(2,1)} %param.19) | copy-start | bytes 2359300
  598.5 5.1 copy-start.59
  598.6 7.9 copy-start.65
  600.6 32.0 %copy-start.48 = (bf16[3,128,768]{2,1,0:T(8,128)(2,1)}, bf16[3,128,768]{2,1,0:T(8,128)(2,1)S(1)}, u32[]{:S(2)}) copy-start(bf16[3,128,768]{2,1,0:T(8,128)(2,1)S(1)} %copy.165) | copy-start | bytes 1769476
  602.6 16.5 copy-start.46
  637.4 2.5 copy-start.36
  639.9 2.3 copy-start.14
  639.9 2.3 copy-start.17
  645.9 2.8 copy-start.47
  645.9 2.8 copy-start.52
  645.9 2.8 copy-start.68
  667.1 5.9 copy-start.9
  675.1 4.9 slice-start.6
  675.6 4.3 slice-start.7
  675.6 16.2 slice-start
  680.0 7.2 copy-start.32
  680.0 11.9 slice-start.1
  680.0 11.9 slice-start.2
  691.9 2.4 copy-start.30
  691.9 16.0 slice-start.3
  694.3 13.6 slice-start.4
  694.3 13.6 slice-start.5
  707.9 2.2 copy-start.74
  707.9 2.4 copy-start.8
  712.6 7.2 copy-start.56
  727.3 3.9 copy-start.69
  738.1 3.8 copy-start.3
  738.1 3.8 copy-start.39
  738.1 3.8 copy-start.40
  744.0 3.0 copy-start.4
  745.8 2.3 copy-start.70
  755.0 2.3 copy-start.37
  755.0 2.3 copy-start.41
  761.2 4.5 copy-start.43
  761.2 4.5 copy-start.53
  768.2 6.3 copy-start.21
  768.8 3.0 copy-start.25
  769.3 3.3 copy-start.27
  769.9 2.7 copy-start.19
  774.0 4.3 copy-start.23
  790.1 3.4 copy-start.34
  805.0 2.6 copy-start.12
  805.0 2.6 copy-start.66
  805.0 4.7 copy-start.13
  805.0 4.7 copy-start.60
  805.1 894.9 %all-reduce.37.cloned.1.call-start = ((), (), s32[]{:S(2)}) async-start(), calls=%async_computation.11 | async-start | bytes 2359296
  1654.0 6.1 copy-start.7
  1654.0 6.1 copy-start.20
  1654.0 65.7 %reduce-scatter.17.cloned.1.call-start = ((), (), s32[]{:S(2)}) async-start(), calls=%async_computation.8 | async-start | bytes 1474560 | tf_op jit(solution)/shard_map/reduce_scatter | solution.py:308
  1659.8 2.5 copy-start.28
  1659.8 88.0 %reduce-scatter.19.cloned.1.call-start = ((), (), s32[]{:S(2)}) async-start(), calls=%async_computation.9 | async-start | bytes 1474560 | tf_op jit(solution)/shard_map/reduce_scatter | solution.py:314
  1660.2 2.1 copy-start.49
  1664.3 2.8 copy-start.35
  1673.1 3.3 copy-start.61
  1673.1 3.3 copy-start.62
  1673.1 76.5 %copy-start.1 = (bf16[512,768]{1,0:T(8,128)(2,1)S(1)}, bf16[512,768]{1,0:T(8,128)(2,1)}, u32[]{:S(2)}) copy-start(bf16[512,768]{1,0:T(8,128)(2,1)} %param.20) | copy-start | bytes 2359300
  (31 other events, 43.7 us)
Sparse Core Ops, SparseCore 0:
  10.9 60.1 all-gather.19
  74.0 56.4 all-gather.15
  133.3 56.1 all-gather.17
  192.3 56.3 all-gather.21
  251.4 80.7 all-gather.23
  334.9 80.8 all-gather.25
  805.2 839.4 all-reduce.34
  1654.2 37.2 all-reduce.36
  1694.1 25.5 reduce-scatter.16
  1722.1 25.6 reduce-scatter.18
where the time goes:
time: 1760 us
  waiting for transfers between devices  824 us (47%)
  blocking collectives  636 us (36%)
  matrix products  141 us (8%)
  local copies, waits for them, and re-layouts  77.6 us (4%)
  other arithmetic  61.4 us (3%)
    unnamed x12, waiting for transfers between devices  786 us
    all_gather x1, blocking collectives, mixed_body(): lax.all_gather(query_bias, ('dp', 'fsdp'), axis=1, tiled=True)  69.5 us
    all_gather x1, blocking collectives, mixed_body(): lax.all_gather(first_shift, ('dp', 'fsdp'), axis=1, tiled=True)  65.9 us
    all_gather x1, blocking collectives, mixed_body(): lax.all_gather(down_bias, ('dp', 'fsdp'), axis=1, tiled=True)  65.5 us
    all_gather x1, blocking collectives, mixed_body(): lax.all_gather(out_bias, ('dp', 'fsdp'), axis=1, tiled=True)  65.4 us
    all_gather x1, blocking collectives, mixed_body(): lax.all_gather(second_shift, ('dp', 'fsdp'), axis=1, tiled=True)  65.3 us
    all_gather x1, blocking collectives, mixed_body(): lax.all_gather(up_bias, ('dp', 'fsdp'), axis=1, tiled=True)  63.5 us
    all_gather x1, blocking collectives, mixed_body(): lax.all_gather(value_bias, ('dp', 'fsdp'), axis=1, tiled=True)  63.2 us
  transfers between devices with their start and end apart: 10, of which 3 were waited for; matrix products, arithmetic and copies ran while one was open for 7% of the time, Pallas kernels for 0%

commit v1 on v0

v1 whole, which is shorter than its diff:
```python
import functools

import jax
import jax.numpy as jnp
import numpy as np
from jax import lax
from jax.experimental import pallas as pl
from jax.experimental.pallas import tpu as pltpu
from jax.sharding import Mesh
from jax.sharding import PartitionSpec as P

HEADS = 12
HEAD_DIM = 64
CAP = 3
LANES = 128
BF16 = jnp.bfloat16
F32 = jnp.float32
NN = (((1,), (0,)), ((), ()))
NT = (((1,), (1,)), ((), ()))
TN = (((0,), (0,)), ((), ()))
SWAP = [(0, 1), (1, 0)]


def dot(a, b, dims=NN):
    return lax.dot_general(a, b, dims, preferred_element_type=F32)


def head_masks():
    lane = lax.broadcasted_iota(jnp.int32, (1, LANES), 1)
    first = (lane < HEAD_DIM).astype(F32).astype(BF16)
    second = (lane >= HEAD_DIM).astype(F32).astype(BF16)
    return first, second


def stacked(two_heads, masks):
    return jnp.concatenate([two_heads * masks[0], two_heads * masks[1]], axis=0)


def side_by_side(rows):
    half = rows.shape[0] // 2
    return jnp.concatenate([rows[:half], rows[half:]], axis=1)


def pair_probs(k_stack, q_pair, length):
    scores = dot(k_stack, q_pair, NT) * HEAD_DIM**-0.5
    keys = k_stack.shape[0] // 2
    scores = scores.reshape(2, keys, scores.shape[1])
    slot = lax.broadcasted_iota(jnp.int32, scores.shape, 1)
    scores = jnp.where(slot < length, scores, -1000000000.0)
    exponent = jnp.exp(scores - jnp.max(scores, axis=1, keepdims=True))
    probs = exponent / jnp.sum(exponent, axis=1, keepdims=True)
    return probs


def attention_kernel(lens_ref, qkv_ref, ctx_ref):
    width = ctx_ref.shape[1]
    length = lens_ref[pl.program_id(0)]
    masks = head_masks()
    for start in range(0, width, LANES):
        q_pair = qkv_ref[:, start : start + LANES]
        k_stack = stacked(qkv_ref[:, width + start : width + start + LANES], masks)
        v_stack = stacked(qkv_ref[:, 2 * width + start : 2 * width + start + LANES], masks)
        probs = pair_probs(k_stack, q_pair, length)
        low = probs.astype(BF16).reshape(k_stack.shape[0], q_pair.shape[0])
        ctx_ref[:, start : start + LANES] = dot(low, v_stack, TN).astype(BF16)


def attention_back_kernel(lens_ref, qkv_ref, dctx_ref, dqkv_ref):
    width = dctx_ref.shape[1]
    length = lens_ref[pl.program_id(0)]
    masks = head_masks()
    scale = HEAD_DIM**-0.5
    for start in range(0, width, LANES):
        q_pair = qkv_ref[:, start : start + LANES]
        k_stack = stacked(qkv_ref[:, width + start : width + start + LANES], masks)
        v_stack = stacked(qkv_ref[:, 2 * width + start : 2 * width + start + LANES], masks)
        d_pair = dctx_ref[:, start : start + LANES]
        probs = pair_probs(k_stack, q_pair, length)
        low = probs.astype(BF16).reshape(k_stack.shape[0], q_pair.shape[0])
        dv = dot(side_by_side(low), stacked(d_pair, masks))
        dprobs = dot(v_stack, d_pair, NT).reshape(probs.shape)
        inner = jnp.sum(dprobs * probs, axis=1, keepdims=True)
        dscores = (probs * (dprobs - inner)).astype(BF16).reshape(low.shape)
        dq = scale * dot(dscores, k_stack, TN)
        dk = scale * dot(side_by_side(dscores), stacked(q_pair, masks))
        dqkv_ref[:, start : start + LANES] = dq.astype(BF16)
        dqkv_ref[:, width + start : width + start + LANES] = dk.astype(BF16)
        dqkv_ref[:, 2 * width + start : 2 * width + start + LANES] = dv.astype(BF16)


def attention(qkv, lens, width):
    chains = lens.shape[0]
    rows = qkv.shape[0] // chains
    return pl.pallas_call(
        attention_kernel,
        out_shape=jax.ShapeDtypeStruct((qkv.shape[0], width), BF16),
        grid_spec=pltpu.PrefetchScalarGridSpec(
            num_scalar_prefetch=1,
            grid=(chains,),
            in_specs=[pl.BlockSpec((rows, 3 * width), lambda i, _: (i, 0))],
            out_specs=pl.BlockSpec((rows, width), lambda i, _: (i, 0)),
        ),
        cost_estimate=pl.CostEstimate(
            flops=8 * qkv.shape[0] * rows * width,
            bytes_accessed=8 * qkv.shape[0] * width,
            transcendentals=qkv.shape[0] * rows * HEADS,
        ),
        name="attention_forward",
    )(lens, qkv)


def attention_back(qkv, dctx, lens):
    chains = lens.shape[0]
    width = dctx.shape[1]
    rows = qkv.shape[0] // chains
    return pl.pallas_call(
        attention_back_kernel,
        out_shape=jax.ShapeDtypeStruct(qkv.shape, BF16),
        grid_spec=pltpu.PrefetchScalarGridSpec(
            num_scalar_prefetch=1,
            grid=(chains,),
            in_specs=[
                pl.BlockSpec((rows, 3 * width), lambda i, _: (i, 0)),
                pl.BlockSpec((rows, width), lambda i, _: (i, 0)),
            ],
            out_specs=pl.BlockSpec((rows, 3 * width), lambda i, _: (i, 0)),
        ),
        cost_estimate=pl.CostEstimate(
            flops=20 * qkv.shape[0] * rows * width,
            bytes_accessed=14 * qkv.shape[0] * width,
            transcendentals=qkv.shape[0] * rows * HEADS,
        ),
        name="attention_backward",
    )(lens, qkv, dctx)


def up_kernel(low_ref, up_ref, bias_ref, active_ref, slope_ref):
    hidden = dot(low_ref[...], up_ref[...]) + bias_ref[...]
    cdf = 0.5 * (1.0 + lax.erf(hidden * (2.0**-0.5)))
    active_ref[...] = (hidden * cdf).astype(BF16)
    density = jnp.exp(-0.5 * hidden * hidden) * ((2.0 * np.pi) ** -0.5)
    slope_ref[...] = (cdf + hidden * density).astype(BF16)


def up_and_gelu(low, up_weight, up_bias):
    rows, width = low.shape
    ff = up_bias.shape[1]
    block = 512
    return pl.pallas_call(
        up_kernel,
        out_shape=[jax.ShapeDtypeStruct((rows, ff), BF16)] * 2,
        grid=(ff // block,),
        in_specs=[
            pl.BlockSpec((rows, width), lambda i: (0, 0)),
            pl.BlockSpec((width, block), lambda i: (0, i)),
            pl.BlockSpec((1, block), lambda i: (0, i)),
        ],
        out_specs=[pl.BlockSpec((rows, block), lambda i: (0, i))] * 2,
        cost_estimate=pl.CostEstimate(
            flops=2 * rows * width * ff,
            bytes_accessed=2 * (rows * width + width * ff + 2 * rows * ff),
            transcendentals=2 * rows * ff,
        ),
        compiler_params=pltpu.CompilerParams(vmem_limit_bytes=40 * 2**20),
        name="up_gelu",
    )(low, up_weight, up_bias)


def normed(values):
    centre = values - jnp.mean(values, axis=-1, keepdims=True)
    root = lax.rsqrt(jnp.mean(centre * centre, axis=-1, keepdims=True) + 1e-05)
    return centre * root, root


def norm_back(grad, unit, root, gain):
    scaled = grad * gain
    inner = jnp.mean(scaled * unit, axis=-1, keepdims=True)
    grad_in = root * (scaled - jnp.mean(scaled, axis=-1, keepdims=True) - unit * inner)
    return grad_in, jnp.sum(grad * unit, axis=0), jnp.sum(grad, axis=0)


class Ring:
    def __init__(self, count):
        depth = 4 if count % 4 == 0 else 2
        wide = count // depth
        order = []
        if wide > 1:
            for z in range(depth):
                ys = range(1, wide) if z % 2 == 0 else reversed(range(1, wide))
                order += [z * wide + y for y in ys]
            order += [z * wide for z in reversed(range(depth))]
        else:
            order = list(range(count))
        self.count = count
        self.pairs = []
        origin = np.zeros((2, count, count), np.int32)
        for core in range(2):
            sign = 1 if core == 0 else -1
            for place, chip in enumerate(order):
                self.pairs.append((core * count + chip, core * count + order[(place + sign) % count]))
                for step in range(count):
                    origin[core, chip, step] = order[(place - sign * step) % count]
        self.origin = origin

    def sources(self):
        table = jnp.asarray(self.origin.reshape(-1))
        at = (lax.axis_index("core") * self.count + lax.axis_index("f")) * self.count
        return [lax.dynamic_index_in_dim(table, at + k, 0, keepdims=False) for k in range(self.count)]

    def pass_on(self, block):
        return lax.ppermute(block, ("core", "f"), self.pairs)


def swap(value, axis):
    return lax.ppermute(value, axis, SWAP)


def pick(value, index, axis):
    return lax.dynamic_index_in_dim(value, index, axis, keepdims=False)


def two_sides(shards, side, groups):
    own = pick(shards, side, 0)
    other = swap(pick(shards, 1 - side, 0), "t")
    place = lax.broadcasted_iota(jnp.int32, (2, 1, 1), 0)
    block = jnp.where(place == side, own[None], other[None])
    if groups > 1:
        return lax.all_gather(block, "r", axis=0, tiled=False)
    return block[None]


def both_cores(own, other, core):
    place = lax.broadcasted_iota(jnp.int32, (1, 1, 2) + (1,) * (own.ndim - 2), 2)
    whole = jnp.where(place == core, own[:, :, None], other[:, :, None])
    return whole.reshape(-1, own.shape[-1])


def ring_gather(blocks, ring, sources):
    held = []
    for block in blocks:
        start = jnp.zeros(block.shape[:2] + (ring.count,) + block.shape[2:], block.dtype)
        held.append(lax.dynamic_update_index_in_dim(start, block, sources[0], 2))
    for step in range(1, ring.count):
        blocks = [ring.pass_on(block) for block in blocks]
        held = [
            lax.dynamic_update_index_in_dim(h, block, sources[step], 2)
            for h, block in zip(held, blocks)
        ]
    return held


def half_sums(grad, groups, ring, core):
    split = grad.reshape(groups, 2, 2, ring.count, -1, grad.shape[-1])
    own = pick(split, core, 2)
    other = swap(pick(split, 1 - core, 2), "core")
    return own, other


def ring_scatter(halves, ring, sources):
    own, other = halves

    def term(step):
        return pick(own, sources[step], 2).astype(F32) + pick(other, sources[step], 2).astype(F32)

    total = term(1)
    for step in range(2, ring.count + 1):
        arrived = ring.pass_on(total.astype(BF16))
        total = arrived.astype(F32) + term(step % ring.count)
    return total


def to_owners(total, side, groups):
    if groups > 1:
        total = lax.psum_scatter(total.astype(BF16), "r", scatter_dimension=0, tiled=True)
    total = total[0]
    own = pick(total, side, 0).astype(F32)
    other = swap(pick(total, 1 - side, 0).astype(BF16), "t").astype(F32)
    place = lax.broadcasted_iota(jnp.int32, (2, 1, 1), 0)
    return jnp.where(place == side, own[None], other[None])


def places(tags, model):
    member = (tags[:, 0] == model).astype(jnp.int32)
    ranking = jnp.cumsum(member) - 1
    slots = lax.broadcasted_iota(jnp.int32, (CAP, member.shape[0]), 0)
    return (slots == ranking[None, :]) & (member[None, :] == 1)


def take(chains, index):
    return jnp.stack([pick(chains, index[s], 0) for s in range(CAP)])


def columns(vectors, extra, rows):
    parts = [v[..., None] for v in vectors]
    if extra is not None:
        parts.append(extra.reshape(extra.shape[:-1] + (rows, -1)))
    block = jnp.concatenate(parts, axis=-1)
    pad = [(0, 0)] * (block.ndim - 1) + [(0, LANES - block.shape[-1])]
    return jnp.pad(block, pad)


def body(ring, groups, *args):
    (
        inputs,
        cotangent,
        lengths,
        tags,
        query_weight,
        query_bias,
        key_weight,
        value_weight,
        value_bias,
        output_projection_weight,
        out_bias,
        first_gain,
        first_shift,
        up_weight,
        up_bias,
        down_weight,
        down_bias,
        second_gain,
        second_shift,
    ) = args
    side, core = lax.axis_index("t"), lax.axis_index("core")
    sources = ring.sources()
    chains = lengths.shape[0]
    width = inputs.shape[1]
    ff = up_weight.shape[2]
    slots = inputs.shape[0] // chains
    shard = query_weight.shape[1]

    attention_shard = jnp.concatenate(
        [
            query_weight,
            key_weight,
            value_weight,
            output_projection_weight,
            columns([query_bias, value_bias, out_bias, first_gain, first_shift], None, shard),
        ],
        axis=-1,
    )
    up_shard = jnp.concatenate(
        [up_weight, columns([down_bias, second_gain, second_shift], up_bias, shard)], axis=-1
    )
    block_a = two_sides(attention_shard, side, groups)
    block_u = two_sides(up_shard, side, groups)
    block_d = two_sides(down_weight, side, groups)

    own_places, other_places = places(tags, side), places(tags, 1 - side)
    order = jnp.arange(chains, dtype=jnp.int32)[None, :]
    own_index = jnp.sum(jnp.where(own_places, order, 0), axis=1)
    other_index = jnp.sum(jnp.where(other_places, order, 0), axis=1)
    own_live, other_live = jnp.any(own_places, axis=1), jnp.any(other_places, axis=1)
    own_len = jnp.sum(jnp.where(own_places, lengths[None, :], 0), axis=1)
    other_len = jnp.sum(jnp.where(other_places, lengths[None, :], 0), axis=1)
    chain_rows = inputs.reshape(chains, slots, width)
    cot_rows = cotangent.reshape(chains, slots, width)
    sent = jnp.concatenate(
        [
            take(chain_rows, other_index).reshape(CAP * slots, width),
            jnp.broadcast_to(jnp.repeat(other_len, 16)[:, None], (CAP * 16, width)).astype(BF16),
        ],
        axis=0,
    )
    arrived = swap(sent, "t")
    rows_in = jnp.concatenate(
        [take(chain_rows, own_index).reshape(CAP * slots, width), arrived[: CAP * slots]], axis=0
    )
    lens = jnp.concatenate(
        [own_len, arrived[CAP * slots :: 16, 0].astype(jnp.int32)]
    )
    own_cot = jnp.where(own_live[:, None, None], take(cot_rows, own_index), 0)
    other_cot = swap(jnp.where(other_live[:, None, None], take(cot_rows, other_index), 0), "t")
    cot = jnp.concatenate([own_cot, other_cot], axis=0).reshape(2 * CAP * slots, width).astype(F32)

    gathered_d = lax.all_gather(
        block_d.reshape(groups * 2, -1, width), "f", axis=1, tiled=True
    ).reshape(groups, 2, -1, width)
    held_a, held_u = ring_gather([block_a, block_u], ring, sources)
    whole_a = both_cores(held_a, swap(held_a, "core"), core)
    whole_u = both_cores(held_u, swap(held_u, "core"), core)
    whole_d = both_cores(gathered_d, swap(gathered_d, "core"), core)

    qkv_weight = whole_a[:, : 3 * width]
    out_weight = whole_a[:, 3 * width : 4 * width]
    small_a = whole_a[:, 4 * width :].astype(F32).T
    small_u = whole_u[:, ff:].astype(F32)
    up_bias_row = small_u[:, 3 : 3 + ff // width].reshape(1, ff)
    small_u = small_u.T
    b_query, b_value, b_out, gain1, shift1 = [small_a[i : i + 1] for i in range(5)]
    b_down, gain2, shift2 = [small_u[i : i + 1] for i in range(3)]

    qkv_bias = jnp.concatenate([b_query, jnp.zeros_like(b_query), b_value], axis=1)
    qkv = (dot(rows_in, qkv_weight) + qkv_bias).astype(BF16)
    context = attention(qkv, lens, width)
    unit1, root1 = normed(rows_in.astype(F32) + dot(context, out_weight) + b_out)
    hidden1 = unit1 * gain1 + shift1
    low1 = hidden1.astype(BF16)
    active, slope = up_and_gelu(low1, whole_u, up_bias_row)
    unit2, root2 = normed(hidden1 + dot(active, whole_d) + b_down)
    result = (unit2 * gain2 + shift2).astype(BF16)

    dr2, g_gain2, g_shift2 = norm_back(cot, unit2, root2, gain2)
    df = dr2.astype(BF16)
    g_down_bias = jnp.sum(df.astype(F32), axis=0)
    g_down = dot(active, df, TN).astype(BF16)
    own_d, other_d = half_sums(g_down, groups, ring, core)
    half_d = (own_d.astype(F32) + other_d.astype(F32)).astype(BF16)
    half_d = jnp.moveaxis(half_d, 2, 0)
    total_d = lax.psum_scatter(
        half_d.reshape(-1, width), "f", scatter_dimension=0, tiled=True
    ).reshape(groups, 2, -1, width)

    du = (dot(df, whole_d, NT) * slope.astype(F32)).astype(BF16)
    g_up_bias = jnp.sum(du.astype(F32), axis=0)
    g_up = jnp.concatenate(
        [
            dot(low1, du, TN).astype(BF16),
            columns([g_down_bias, g_gain2, g_shift2], g_up_bias, width).astype(BF16),
        ],
        axis=1,
    )
    total_u = ring_scatter(half_sums(g_up, groups, ring, core), ring, sources)
    dh1 = dr2 + dot(du, whole_u[:, :ff], NT)
    dr1, g_gain1, g_shift1 = norm_back(dh1, unit1, root1, gain1)
    da = dr1.astype(BF16)
    g_out_bias = jnp.sum(da.astype(F32), axis=0)
    g_out = dot(context, da, TN)
    dctx = dot(da, out_weight, NT).astype(BF16)
    dqkv = attention_back(qkv, dctx, lens)
    g_qkv_bias = jnp.sum(dqkv.astype(F32), axis=0)
    g_attention = jnp.concatenate(
        [
            dot(rows_in, dqkv, TN).astype(BF16),
            g_out.astype(BF16),
            columns(
                [g_qkv_bias[:width], g_qkv_bias[2 * width :], g_out_bias, g_gain1, g_shift1],
                None,
                width,
            ).astype(BF16),
        ],
        axis=1,
    )
    total_a = ring_scatter(half_sums(g_attention, groups, ring, core), ring, sources)
    rows_grad = (dr1 + dot(dqkv, qkv_weight, NT)).astype(BF16)

    grads_d = to_owners(total_d, side, groups)
    grads_u = to_owners(total_u, side, groups)
    grads_a = to_owners(total_a, side, groups)

    own_rank = jnp.sum(jnp.where(own_places, order_of(CAP), 0), axis=0)
    other_rank = jnp.sum(jnp.where(other_places, order_of(CAP), 0), axis=0)

    def home(values):
        values = values.reshape(2, CAP, slots, width)
        back = swap(values[1], "t")
        out = [
            jnp.where(
                tags[i, 0] == side, pick(values[0], own_rank[i], 0), pick(back, other_rank[i], 0)
            )
            for i in range(chains)
        ]
        return jnp.concatenate(out, axis=0)

    small_a = grads_a[:, :, 4 * width :]
    small_u = grads_u[:, :, ff:]
    return (
        home(result),
        home(rows_grad),
        grads_a[:, :, :width],
        small_a[:, :, 0],
        grads_a[:, :, width : 2 * width],
        grads_a[:, :, 2 * width : 3 * width],
        small_a[:, :, 1],
        grads_a[:, :, 3 * width : 4 * width],
        small_a[:, :, 2],
        small_a[:, :, 3],
        small_a[:, :, 4],
        grads_u[:, :, :ff],
        small_u[:, :, 3 : 3 + ff // width].reshape(2, -1),
        grads_d,
        small_u[:, :, 0],
        small_u[:, :, 1],
        small_u[:, :, 2],
    )


def order_of(count):
    return jnp.arange(count, dtype=jnp.int32)[:, None]


def solution(mesh):
    dp, fsdp = mesh.shape["dp"], mesh.shape["fsdp"]
    groups = dp // 4
    inner = Mesh(mesh.devices.reshape(groups, 2, 2, fsdp), ("r", "t", "core", "f"))
    every = ("r", "t", "core", "f")
    rows, vector, matrix = P(every, None), P(None, every), P(None, every, None)
    weights = (
        matrix,
        vector,
        matrix,
        matrix,
        vector,
        matrix,
        vector,
        vector,
        vector,
        matrix,
        vector,
        matrix,
        vector,
        vector,
        vector,
    )
    return jax.shard_map(
        functools.partial(body, Ring(fsdp), groups),
        mesh=inner,
        in_specs=(rows, rows, P(every), rows) + weights,
        out_specs=(rows, rows) + weights,
        check_vma=False,
    )
```

time: 1760 us -> 459 us (0.26)
  waiting for transfers between devices: 824 us -> 132 us
  blocking collectives: 636 us -> 0 us
  matrix products: 141 us -> 59.6 us
  starting transfers between devices: 0.85 us -> 49.3 us
  between operations: 16.2 us -> 60.5 us
  Pallas kernels: 0 us -> 34.9 us
  local copies, waits for them, and re-layouts: 77.6 us -> 57.7 us
    unnamed x12 -> x2, waiting for transfers between devices: 786 us -> 0.03 us
    all_gather x9 -> x0, blocking collectives: 585 us -> none  [the longest x1 69.5 us: mixed_body(): lax.all_gather(query_bias, ('dp', 'fsdp'), axis=1, tiled=True)]
    ppermute x0 -> x44, waiting for transfers between devices: none -> 132 us  [the longest x28 102 us: pass_on(): return lax.ppermute(block, ('core', 'f'), self.pairs)]
    dot_general x56 -> x11, matrix products: 141 us -> 59.6 us  [dot(): return lax.dot_general(a, b, dims, preferred_element_type=F32)]
    unnamed x2 -> x0, blocking collectives: 51.9 us -> none
    ppermute x0 -> x44, starting transfers between devices: none -> 49.2 us  [the longest x28 37.6 us: pass_on(): return lax.ppermute(block, ('core', 'f'), self.pairs)]
    reduce_scatter x2 -> x1, waiting for transfers between devices: 37.2 us -> 0.01 us  [body(): lax.psum_scatter(half_d.reshape(-1, width), 'f', scatter_dimension=0, til...]
    pallas_call x0 -> x3, Pallas kernels: none -> 34.9 us  [the longest x1 16.1 us: attention_back(): pl.pallas_call(attention_back_kernel, out_shape=jax.ShapeDtypeStruct(qkv....]
  transfers between devices with their start and end apart: 10 -> 46, of which waited for: 3 -> 30; matrix products, arithmetic and copies ran while one was open for 7% -> 24% of each run, Pallas kernels for 0% -> 8%
where the time goes in v1:
time: 459 us; the launch traced here: 453 us
  waiting for transfers between devices  132 us (29%)
  between operations  60.5 us (13%)
  matrix products  59.6 us (13%)
  other arithmetic  58.9 us (13%)
  local copies, waits for them, and re-layouts  57.7 us (13%)
  starting transfers between devices  49.3 us (11%)
  Pallas kernels  34.9 us (8%)
    ppermute x28, waiting for transfers between devices, pass_on(): return lax.ppermute(block, ('core', 'f'), self.pairs)  102 us
    dot_general x11, matrix products, dot(): return lax.dot_general(a, b, dims, preferred_element_type=F32)  59.6 us
    ppermute x28, starting transfers between devices, pass_on(): return lax.ppermute(block, ('core', 'f'), self.pairs)  37.6 us
    ppermute x16, waiting for transfers between devices, swap(): return lax.ppermute(value, axis, SWAP)  29.6 us
    unnamed x80, local copies, waits for them, and re-layouts  17.2 us
    convert_element_type x14, other arithmetic, ring_scatter(): arrived = ring.pass_on(total.astype(BF16))  16.5 us
    pallas_call x1, Pallas kernels, attention_back(): pl.pallas_call(attention_back_kernel, out_shape=jax.ShapeDtypeStruct(qkv....  16.1 us
    ppermute x16, starting transfers between devices, swap(): return lax.ppermute(value, axis, SWAP)  11.6 us
  transfers between devices with their start and end apart: 46, of which 30 were waited for; matrix products, arithmetic and copies ran while one was open for 24% of the time, Pallas kernels for 8%

profile of v1, /device:TPU:0, one launch (start us, length us, event | category | flops | bytes accessed | tf_op | source)
XLA Modules:
  0.0 453.1 jit_solution(17375647856559659524)
XLA Ops:
  10.0 3.0 collective-permute-start.10
  20.2 2.1 collective-permute-start.19
  48.4 2.0 collective-permute-done.2
  50.4 2.5 collective-permute-start.3
  53.7 5.7 %collective-permute-done.12 = bf16[1,2,24,3200]{3,2,1,0:T(8,128)(2,1)S(1)} collective-permute-done((bf16[1,2,24,3200]{3,2,1,0:T(8,128)(2,1)S(1)}, bf16[1,2,24,3200]{3,2,1,0:T(8,128)(2,1)S(1)}, u32[]{:S(2)}, u32[]{:S(2)}) %collective-permute-start.12) | collective-permute-done | bytes 307232 | tf_op jit(solution)/shard_map/ppermute | solution.py:211
  59.4 1.9 collective-permute-start.13
  61.3 5.3 %collective-permute-done.3 = bf16[1,2,24,3200]{3,2,1,0:T(8,128)(2,1)S(1)} collective-permute-done((bf16[1,2,24,3200]{3,2,1,0:T(8,128)(2,1)S(1)}, bf16[1,2,24,3200]{3,2,1,0:T(8,128)(2,1)S(1)}, u32[]{:S(2)}, u32[]{:S(2)}) %collective-permute-start.3) | collective-permute-done | bytes 307232 | tf_op jit(solution)/shard_map/ppermute | solution.py:211
  67.7 2.1 collective-permute-done.13
  70.2 3.8 collective-permute-done.4
  74.0 2.0 collective-permute-start.5
  76.7 13.5 %collective-permute-done.14 = bf16[1,2,24,3200]{3,2,1,0:T(8,128)(2,1)S(1)} collective-permute-done((bf16[1,2,24,3200]{3,2,1,0:T(8,128)(2,1)S(1)}, bf16[1,2,24,3200]{3,2,1,0:T(8,128)(2,1)S(1)}, u32[]{:S(2)}, u32[]{:S(2)}) %collective-permute-start.14) | collective-permute-done | bytes 307232 | tf_op jit(solution)/shard_map/ppermute | solution.py:211
  90.3 8.7 %collective-permute-done.5 = bf16[1,2,24,3200]{3,2,1,0:T(8,128)(2,1)S(1)} collective-permute-done((bf16[1,2,24,3200]{3,2,1,0:T(8,128)(2,1)S(1)}, bf16[1,2,24,3200]{3,2,1,0:T(8,128)(2,1)S(1)}, u32[]{:S(2)}, u32[]{:S(2)}) %collective-permute-start.5) | collective-permute-done | bytes 307232 | tf_op jit(solution)/shard_map/ppermute | solution.py:211
  99.8 2.5 collective-permute-done.15
  102.9 2.9 collective-permute-done.6
  107.0 2.1 collective-permute-done.16
  109.7 2.9 collective-permute-done.7
  114.0 1.9 collective-permute-done.17
  116.1 3.7 collective-permute-done.8
  138.0 2.0 collective-permute-start.22
  140.3 1.8 pad_maximum_fusion.6
  142.1 2.1 fusion.77
  144.2 22.1 %collective-permute-done.22 = bf16[3,128,768]{2,1,0:T(8,128)(2,1)S(1)} collective-permute-done((bf16[3,128,768]{2,1,0:T(8,128)(2,1)}, bf16[3,128,768]{2,1,0:T(8,128)(2,1)S(1)}, u32[]{:S(2)}, u32[]{:S(2)}) %collective-permute-start.22) | collective-permute-done | bytes 589856 | tf_op jit(solution)/shard_map/ppermute | solution.py:215
  167.4 1.9 slice.257
  170.0 4.5 %bitcast_select_fusion = (bf16[768,3200]{1,0:T(8,128)(2,1)S(1)}, bf16[768,3200]{1,0:T(8,128)(2,1)S(1)}) fusion(pred[768]{0:T(1024)(128)(4,1)S(1)} %broadcast_in_dim.455, bf16[2,8,24,3200]{3,2,1,0:T(8,128)(2,1)} %bitcast.68, bf16[2,8,24,3200]{3,2,1,0:T(8,128)(2,1)S(1)} %bitcast.364, bf16[2,8,24,3200]{3,2,1,0:T(8,128)(2,1)} %bitcast.45, ...), kind=kLoop, calls=%fused_computation.9 | loop fusion | flops 4915200 | bytes 19661568 | tf_op jit(solution)/shard_map/jit(_where)/select_n | solution.py:234
  178.7 6.9 %add_convert_fusion.qkv_ref = bf16[768,2304]{1,0:T(8,128)(2,1)} fusion(f32[2304]{0:T(1024)S(1)} %fusion.67, bf16[768,3200]{1,0:T(8,128)(2,1)} %copy-done.5, bf16[384,768]{1,0:T(8,128)(2,1)} %slice.257, bf16[384,768]{1,0:T(8,128)(2,1)S(1)} %bitcast.375), kind=kOutput, calls=%fused_computation.3 | convolution fusion | flops 2723807232 | bytes 8266752 | tf_op jit(solution)/shard_map/dot_general | solution.py:25
  186.1 8.6 %attention_forward.1 = bf16[768,768]{1,0:T(8,128)(2,1)} custom-call(s32[6]{0:T(128)} %pad_add_fusion.lens_ref, bf16[768,2304]{1,0:T(8,128)(2,1)} %add_convert_fusion.qkv_ref), custom_call_target="tpu_custom_call" | custom-call | flops 603979776 | bytes 4718592 | tf_op jit(solution)/shard_map/attention_forward/pallas_call | solution.py:94
  196.2 2.5 fusion.92
  199.6 10.3 %up_gelu.1 = (bf16[768,3072]{1,0:T(8,128)(2,1)S(1)}, bf16[768,3072]{1,0:T(8,128)(2,1)S(1)}) custom-call(bf16[768,768]{1,0:T(8,128)(2,1)S(1)} %fusion.15.low_ref, bf16[768,3200]{1,0:T(8,128)(2,1)} %copy-done.6, f32[1,3072]{1,0:T(1,128)S(1)} %reshape.883.bias_ref), custom_call_target="tpu_custom_call" | custom-call | flops 3623878656 | bytes 15335424 | tf_op jit(solution)/shard_map/up_gelu/pallas_call | solution.py:149
  209.9 4.5 %bitcast_select_fusion.2 = bf16[3072,768]{1,0:T(8,128)(2,1)} fusion(pred[3072]{0:T(1024)(128)(4,1)S(1)} %broadcast_in_dim.505, bf16[2,768,768]{2,1,0:T(8,128)(2,1)} %bitcast.74, bf16[2,768,768]{2,1,0:T(8,128)(2,1)S(1)} %copy-done.12), kind=kLoop, calls=%fused_computation.15 | loop fusion | flops 2359296 | bytes 9440256 | tf_op jit(solution)/shard_map/jit(_where)/select_n | solution.py:234
  214.5 6.5 %fusion.93 = (f32[768]{0:T(1024)S(1)}, f32[768,768]{1,0:T(8,128)S(1)}) fusion(f32[768]{0:T(1024)S(1)} %get-tuple-element.37, bf16[768,3072]{1,0:T(8,128)(2,1)S(1)} %get-tuple-element.19, bf16[3072,768]{1,0:T(8,128)(2,1)} %bitcast_select_fusion.2, f32[768]{0:T(1024)S(1)} %get-tuple-element.39, f32[768]{0:T(1024)S(1)} %get-tuple-element.38, ...), kind=kOutput, calls=%fused_computation.258 | convolution fusion | flops 3628006656 | bytes 14174208 | tf_op jit(solution)/shard_map/dot_general | solution.py:25
  222.7 2.3 convert_reduce_fusion.2
  224.9 9.3 %fusion.94 = (bf16[3072]{0:T(1024)(128)(2,1)S(1)}, bf16[768,3072]{1,0:T(8,128)(2,1)}) fusion(bf16[768,3072]{1,0:T(8,128)(2,1)S(1)} %get-tuple-element.20, bf16[3072,768]{1,0:T(8,128)(2,1)} %bitcast_select_fusion.2, f32[768,768]{1,0:T(8,128)} %get-tuple-element.48), kind=kOutput, calls=%fused_computation.259 | convolution fusion | flops 3633902592 | bytes 16521216 | tf_op jit(solution)/shard_map/dot_general | solution.py:25
  234.2 9.1 %multiply_reduce_fusion = (bf16[768]{0:T(1024)(128)(2,1)}, f32[768]{0:T(1024)S(1)}, f32[768]{0:T(1024)S(1)}, bf16[768]{0:T(1024)(128)(2,1)}, f32[768,768]{1,0:T(8,128)S(1)}) fusion(f32[768,768]{1,0:T(8,128)S(1)} %get-tuple-element.141, f32[768]{0:T(1024)S(1)} %add_rsqrt_fusion.1, f32[768]{0:T(1024)S(1)} %broadcast_multiply_fusion.4, ...), kind=kOutput, calls=%fused_computation.33 | convolution fusion | flops 3629773824 | bytes 16533504 | tf_op jit(solution)/shard_map/dot_general | solution.py:25
  243.3 5.7 %convolution_convert_fusion.2 = bf16[768,3072]{1,0:T(8,128)(2,1)} fusion(bf16[768,768]{1,0:T(8,128)(2,1)S(1)} %fusion.15.low_ref, bf16[768,3072]{1,0:T(8,128)(2,1)S(1)} %copy-done.32), kind=kOutput, calls=%fused_computation.6 | convolution fusion | flops 3626237952 | bytes 10616832 | tf_op jit(solution)/shard_map/dot_general | solution.py:25
  249.9 4.3 convolution_convert_fusion.4.dctx_ref
  254.2 2.2 convolution_convert_fusion.3
  256.4 5.9 %convolution_convert_fusion.1 = bf16[3072,768]{1,0:T(8,128)(2,1)} fusion(bf16[768,3072]{1,0:T(8,128)(2,1)S(1)} %get-tuple-element.19, f32[768,768]{1,0:T(8,128)S(1)} %copy-done.11), kind=kOutput, calls=%fused_computation.5 | convolution fusion | flops 3626827776 | bytes 11796480 | tf_op jit(solution)/shard_map/dot_general | solution.py:25
  263.6 16.1 %attention_backward.1 = bf16[768,2304]{1,0:T(8,128)(2,1)} custom-call(s32[6]{0:T(128)} %pad_add_fusion.lens_ref, bf16[768,2304]{1,0:T(8,128)(2,1)} %add_convert_fusion.qkv_ref, bf16[768,768]{1,0:T(8,128)(2,1)} %convolution_convert_fusion.4.dctx_ref), custom_call_target="tpu_custom_call" | custom-call | flops 1509949440 | bytes 8257536 | tf_op jit(solution)/shard_map/attention_backward/pallas_call | solution.py:116
  280.7 2.7 pad_maximum_fusion
  285.1 2.0 copy-done
  288.4 4.4 convolution_convert_fusion
  299.2 4.3 constant_dynamic-slice_fusion.9
  308.3 1.7 copy-done.1
  310.6 3.0 add_convert_fusion.1
  313.7 1.8 collective-permute-start.23
  339.7 3.8 fusion.4
  346.5 2.5 collective-permute-start.25
  349.0 2.8 collective-permute-done.34
  353.6 5.2 %collective-permute-done.25 = bf16[1,2,24,3200]{3,2,1,0:T(8,128)(2,1)S(1)} collective-permute-done((bf16[1,2,24,3200]{3,2,1,0:T(8,128)(2,1)S(1)}, bf16[1,2,24,3200]{3,2,1,0:T(8,128)(2,1)S(1)}, u32[]{:S(2)}, u32[]{:S(2)}) %collective-permute-start.25) | collective-permute-done | bytes 307232 | tf_op jit(solution)/shard_map/ppermute | solution.py:211
  360.0 2.0 collective-permute-start.26
  362.0 6.5 %collective-permute-done.35 = bf16[1,2,24,3200]{3,2,1,0:T(8,128)(2,1)S(1)} collective-permute-done((bf16[1,2,24,3200]{3,2,1,0:T(8,128)(2,1)S(1)}, bf16[1,2,24,3200]{3,2,1,0:T(8,128)(2,1)S(1)}, u32[]{:S(2)}, u32[]{:S(2)}) %collective-permute-start.35) | collective-permute-done | bytes 307232 | tf_op jit(solution)/shard_map/ppermute | solution.py:211
  369.6 2.2 collective-permute-start.36
  371.8 7.0 %collective-permute-done.26 = bf16[1,2,24,3200]{3,2,1,0:T(8,128)(2,1)S(1)} collective-permute-done((bf16[1,2,24,3200]{3,2,1,0:T(8,128)(2,1)S(1)}, bf16[1,2,24,3200]{3,2,1,0:T(8,128)(2,1)S(1)}, u32[]{:S(2)}, u32[]{:S(2)}) %collective-permute-start.26) | collective-permute-done | bytes 307232 | tf_op jit(solution)/shard_map/ppermute | solution.py:211
  381.7 2.2 collective-permute-done.36
  388.4 2.0 collective-permute-start.28
  393.2 2.3 collective-permute-start.38
  397.6 2.5 collective-permute-start.29
  401.3 2.3 collective-permute-start.39
  406.1 2.5 collective-permute-start.30
  408.6 3.6 collective-permute-done.39
  415.1 5.9 %collective-permute-done.30 = bf16[1,2,24,3200]{3,2,1,0:T(8,128)(2,1)S(1)} collective-permute-done((bf16[1,2,24,3200]{3,2,1,0:T(8,128)(2,1)S(1)}, bf16[1,2,24,3200]{3,2,1,0:T(8,128)(2,1)S(1)}, u32[]{:S(2)}, u32[]{:S(2)}) %collective-permute-start.30) | collective-permute-done | bytes 307232 | tf_op jit(solution)/shard_map/ppermute | solution.py:211
  426.1 3.9 collective-permute-done.31
  432.3 5.4 %collective-permute-done.32 = bf16[24,3200]{1,0:T(8,128)(2,1)S(1)} collective-permute-done((bf16[24,3200]{1,0:T(8,128)(2,1)S(1)}, bf16[24,3200]{1,0:T(8,128)(2,1)S(1)}, u32[]{:S(2)}, u32[]{:S(2)}) %collective-permute-start.32) | collective-permute-done | bytes 153632 | tf_op jit(solution)/shard_map/ppermute | solution.py:215
  443.0 2.1 collective-permute-done.43
  (276 shorter events, 108.9 us)
Async XLA Ops:
  7.2 15.2 %copy-start.26 = (s32[128]{0:T(128)S(1)}, s32[128]{0:T(128)}, u32[]{:S(2)}) copy-start(s32[128]{0:T(128)} %constant.757.clone) | copy-start | bytes 1540
  7.2 12.9 %copy-start.25 = (bf16[2,96,768]{2,1,0:T(8,128)(2,1)S(1)}, bf16[2,96,768]{2,1,0:T(8,128)(2,1)}, u32[]{:S(2)}) copy-start(bf16[2,96,768]{2,1,0:T(8,128)(2,1)} %param.35) | copy-start | bytes 884740
  7.2 15.0 %copy-start.27 = (s32[4,1]{0,1:T(1,128)S(1)}, s32[4,1]{0,1:T(1,128)}, u32[]{:S(2)}) copy-start(s32[4,1]{0,1:T(1,128)} %param.23) | copy-start | bytes 52
  7.2 162.8 %all-gather.2.cloned.1.call-start = ((), (), s32[]{:S(2)}) async-start(), calls=%async_computation.1 | async-start | bytes 2654208 | tf_op jit(solution)/shard_map/all_gather | solution.py:376
  10.0 29.7 %collective-permute-start.10 = (bf16[24,3200]{1,0:T(8,128)(2,1)S(1)}, bf16[24,3200]{1,0:T(8,128)(2,1)S(1)}, u32[]{:S(2)}, u32[]{:S(2)}) collective-permute-start(bf16[24,3200]{1,0:T(8,128)(2,1)S(1)} %get-tuple-element.97), channel_id=1, source_target_pairs={{0,16},{16,0},{1,17},{17,1},{2,18},{18,2},{3,19},{19,3},{4,20},{20... | collective-permute-start | bytes 460808 | tf_op jit(solution)/shard_map/ppermute | solution.py:215
  20.0 19.6 %collective-permute-start.1 = (bf16[24,3200]{1,0:T(8,128)(2,1)S(1)}, bf16[24,3200]{1,0:T(8,128)(2,1)S(1)}, u32[]{:S(2)}, u32[]{:S(2)}) collective-permute-start(bf16[24,3200]{1,0:T(8,128)(2,1)S(1)} %get-tuple-element.99), channel_id=1, source_target_pairs={{0,16},{16,0},{1,17},{17,1},{2,18},{18,2},{3,19},{19,3},{4,20},{20... | collective-permute-start | bytes 460808 | tf_op jit(solution)/shard_map/ppermute | solution.py:215
  20.2 18.6 %collective-permute-start.19 = (bf16[96,768]{1,0:T(8,128)(2,1)S(1)}, bf16[96,768]{1,0:T(8,128)(2,1)S(1)}, u32[]{:S(2)}, u32[]{:S(2)}) collective-permute-start(bf16[96,768]{1,0:T(8,128)(2,1)S(1)} %get-tuple-element.103), channel_id=1, source_target_pairs={{0,16},{16,0},{1,17},{17,1},{2,18},{18,2},{3,19},{19,3},{4,20},{20... | collective-permute-start | bytes 442376 | tf_op jit(solution)/shard_map/ppermute | solution.py:215
  39.6 399.2 %reduce-scatter.2.cloned.1.call-start = ((), (), s32[]{:S(2)}) async-start(), calls=%async_computation.2 | async-start | bytes 2654208 | tf_op jit(solution)/shard_map/reduce_scatter | solution.py:410
  40.0 6.9 %collective-permute-start.11 = (bf16[1,2,24,3200]{3,2,1,0:T(8,128)(2,1)S(1)}, bf16[1,2,24,3200]{3,2,1,0:T(8,128)(2,1)S(1)}, u32[]{:S(2)}, u32[]{:S(2)}) collective-permute-start(bf16[1,2,24,3200]{3,2,1,0:T(8,128)(2,1)S(1)} %get-tuple-element.122), channel_id=1, source_target_pairs={{1,3},{3,5},{5,7},{7,6},{6,4},{4,2},{2,0},{0,1},{9,8},{11,9},{13,1... | collective-permute-start | bytes 921608 | tf_op jit(solution)/shard_map/ppermute | solution.py:211
  41.6 8.8 %collective-permute-start.2 = (bf16[1,2,24,3200]{3,2,1,0:T(8,128)(2,1)S(1)}, bf16[1,2,24,3200]{3,2,1,0:T(8,128)(2,1)S(1)}, u32[]{:S(2)}, u32[]{:S(2)}) collective-permute-start(bf16[1,2,24,3200]{3,2,1,0:T(8,128)(2,1)S(1)} %get-tuple-element.123), channel_id=1, source_target_pairs={{1,3},{3,5},{5,7},{7,6},{6,4},{4,2},{2,0},{0,1},{9,8},{11,9},{13,1... | collective-permute-start | bytes 921608 | tf_op jit(solution)/shard_map/ppermute | solution.py:211
  46.9 12.4 %collective-permute-start.12 = (bf16[1,2,24,3200]{3,2,1,0:T(8,128)(2,1)S(1)}, bf16[1,2,24,3200]{3,2,1,0:T(8,128)(2,1)S(1)}, u32[]{:S(2)}, u32[]{:S(2)}) collective-permute-start(bf16[1,2,24,3200]{3,2,1,0:T(8,128)(2,1)S(1)} %collective-permute-done.11), channel_id=1, source_target_pairs={{1,3},{3,5},{5,7},{7,6},{6,4},{4,2},{2,0},{0,1},{9,8},{11,9},{13,1... | collective-permute-start | bytes 921608 | tf_op jit(solution)/shard_map/ppermute | solution.py:211
  50.4 16.2 %collective-permute-start.3 = (bf16[1,2,24,3200]{3,2,1,0:T(8,128)(2,1)S(1)}, bf16[1,2,24,3200]{3,2,1,0:T(8,128)(2,1)S(1)}, u32[]{:S(2)}, u32[]{:S(2)}) collective-permute-start(bf16[1,2,24,3200]{3,2,1,0:T(8,128)(2,1)S(1)} %collective-permute-done.2), channel_id=1, source_target_pairs={{1,3},{3,5},{5,7},{7,6},{6,4},{4,2},{2,0},{0,1},{9,8},{11,9},{13,1... | collective-permute-start | bytes 921608 | tf_op jit(solution)/shard_map/ppermute | solution.py:211
  59.4 10.5 %collective-permute-start.13 = (bf16[1,2,24,3200]{3,2,1,0:T(8,128)(2,1)S(1)}, bf16[1,2,24,3200]{3,2,1,0:T(8,128)(2,1)S(1)}, u32[]{:S(2)}, u32[]{:S(2)}) collective-permute-start(bf16[1,2,24,3200]{3,2,1,0:T(8,128)(2,1)S(1)} %collective-permute-done.12), channel_id=1, source_target_pairs={{1,3},{3,5},{5,7},{7,6},{6,4},{4,2},{2,0},{0,1},{9,8},{11,9},{13,1... | collective-permute-start | bytes 921608 | tf_op jit(solution)/shard_map/ppermute | solution.py:211
  66.6 7.4 %collective-permute-start.4 = (bf16[1,2,24,3200]{3,2,1,0:T(8,128)(2,1)S(1)}, bf16[1,2,24,3200]{3,2,1,0:T(8,128)(2,1)S(1)}, u32[]{:S(2)}, u32[]{:S(2)}) collective-permute-start(bf16[1,2,24,3200]{3,2,1,0:T(8,128)(2,1)S(1)} %collective-permute-done.3), channel_id=1, source_target_pairs={{1,3},{3,5},{5,7},{7,6},{6,4},{4,2},{2,0},{0,1},{9,8},{11,9},{13,1... | collective-permute-start | bytes 921608 | tf_op jit(solution)/shard_map/ppermute | solution.py:211
  69.8 20.4 %collective-permute-start.14 = (bf16[1,2,24,3200]{3,2,1,0:T(8,128)(2,1)S(1)}, bf16[1,2,24,3200]{3,2,1,0:T(8,128)(2,1)S(1)}, u32[]{:S(2)}, u32[]{:S(2)}) collective-permute-start(bf16[1,2,24,3200]{3,2,1,0:T(8,128)(2,1)S(1)} %collective-permute-done.13), channel_id=1, source_target_pairs={{1,3},{3,5},{5,7},{7,6},{6,4},{4,2},{2,0},{0,1},{9,8},{11,9},{13,1... | collective-permute-start | bytes 921608 | tf_op jit(solution)/shard_map/ppermute | solution.py:211
  74.0 25.0 %collective-permute-start.5 = (bf16[1,2,24,3200]{3,2,1,0:T(8,128)(2,1)S(1)}, bf16[1,2,24,3200]{3,2,1,0:T(8,128)(2,1)S(1)}, u32[]{:S(2)}, u32[]{:S(2)}) collective-permute-start(bf16[1,2,24,3200]{3,2,1,0:T(8,128)(2,1)S(1)} %collective-permute-done.4), channel_id=1, source_target_pairs={{1,3},{3,5},{5,7},{7,6},{6,4},{4,2},{2,0},{0,1},{9,8},{11,9},{13,1... | collective-permute-start | bytes 921608 | tf_op jit(solution)/shard_map/ppermute | solution.py:211
  76.7 43.9 %copy-start.31 = (s32[4]{0:T(128)S(1)}, s32[4]{0:T(128)}, u32[]{:S(2)}) copy-start(s32[4]{0:T(128)} %param.22) | copy-start | bytes 52
  76.7 57.5 %copy-start.13 = (bf16[512,768]{1,0:T(8,128)(2,1)S(1)}, bf16[512,768]{1,0:T(8,128)(2,1)}, u32[]{:S(2)}) copy-start(bf16[512,768]{1,0:T(8,128)(2,1)} %param.20) | copy-start | bytes 2359300
  90.3 12.0 %collective-permute-start.15 = (bf16[1,2,24,3200]{3,2,1,0:T(8,128)(2,1)S(1)}, bf16[1,2,24,3200]{3,2,1,0:T(8,128)(2,1)S(1)}, u32[]{:S(2)}, u32[]{:S(2)}) collective-permute-start(bf16[1,2,24,3200]{3,2,1,0:T(8,128)(2,1)S(1)} %collective-permute-done.14), channel_id=1, source_target_pairs={{1,3},{3,5},{5,7},{7,6},{6,4},{4,2},{2,0},{0,1},{9,8},{11,9},{13,1... | collective-permute-start | bytes 921608 | tf_op jit(solution)/shard_map/ppermute | solution.py:211
  99.0 6.9 %collective-permute-start.6 = (bf16[1,2,24,3200]{3,2,1,0:T(8,128)(2,1)S(1)}, bf16[1,2,24,3200]{3,2,1,0:T(8,128)(2,1)S(1)}, u32[]{:S(2)}, u32[]{:S(2)}) collective-permute-start(bf16[1,2,24,3200]{3,2,1,0:T(8,128)(2,1)S(1)} %collective-permute-done.5), channel_id=1, source_target_pairs={{1,3},{3,5},{5,7},{7,6},{6,4},{4,2},{2,0},{0,1},{9,8},{11,9},{13,1... | collective-permute-start | bytes 921608 | tf_op jit(solution)/shard_map/ppermute | solution.py:211
  102.2 6.9 %collective-permute-start.16 = (bf16[1,2,24,3200]{3,2,1,0:T(8,128)(2,1)S(1)}, bf16[1,2,24,3200]{3,2,1,0:T(8,128)(2,1)S(1)}, u32[]{:S(2)}, u32[]{:S(2)}) collective-permute-start(bf16[1,2,24,3200]{3,2,1,0:T(8,128)(2,1)S(1)} %collective-permute-done.15), channel_id=1, source_target_pairs={{1,3},{3,5},{5,7},{7,6},{6,4},{4,2},{2,0},{0,1},{9,8},{11,9},{13,1... | collective-permute-start | bytes 921608 | tf_op jit(solution)/shard_map/ppermute | solution.py:211
  105.8 6.9 %collective-permute-start.7 = (bf16[1,2,24,3200]{3,2,1,0:T(8,128)(2,1)S(1)}, bf16[1,2,24,3200]{3,2,1,0:T(8,128)(2,1)S(1)}, u32[]{:S(2)}, u32[]{:S(2)}) collective-permute-start(bf16[1,2,24,3200]{3,2,1,0:T(8,128)(2,1)S(1)} %collective-permute-done.6), channel_id=1, source_target_pairs={{1,3},{3,5},{5,7},{7,6},{6,4},{4,2},{2,0},{0,1},{9,8},{11,9},{13,1... | collective-permute-start | bytes 921608 | tf_op jit(solution)/shard_map/ppermute | solution.py:211
  109.1 6.9 %collective-permute-start.17 = (bf16[1,2,24,3200]{3,2,1,0:T(8,128)(2,1)S(1)}, bf16[1,2,24,3200]{3,2,1,0:T(8,128)(2,1)S(1)}, u32[]{:S(2)}, u32[]{:S(2)}) collective-permute-start(bf16[1,2,24,3200]{3,2,1,0:T(8,128)(2,1)S(1)} %collective-permute-done.16), channel_id=1, source_target_pairs={{1,3},{3,5},{5,7},{7,6},{6,4},{4,2},{2,0},{0,1},{9,8},{11,9},{13,1... | collective-permute-start | bytes 921608 | tf_op jit(solution)/shard_map/ppermute | solution.py:211
  112.7 7.1 %collective-permute-start.8 = (bf16[1,2,24,3200]{3,2,1,0:T(8,128)(2,1)S(1)}, bf16[1,2,24,3200]{3,2,1,0:T(8,128)(2,1)S(1)}, u32[]{:S(2)}, u32[]{:S(2)}) collective-permute-start(bf16[1,2,24,3200]{3,2,1,0:T(8,128)(2,1)S(1)} %collective-permute-done.7), channel_id=1, source_target_pairs={{1,3},{3,5},{5,7},{7,6},{6,4},{4,2},{2,0},{0,1},{9,8},{11,9},{13,1... | collective-permute-start | bytes 921608 | tf_op jit(solution)/shard_map/ppermute | solution.py:211
  116.0 54.0 %collective-permute-start.18 = (bf16[1,2,8,24,3200]{4,3,2,1,0:T(8,128)(2,1)S(1)}, bf16[1,2,8,24,3200]{4,3,2,1,0:T(8,128)(2,1)}, u32[]{:S(2)}, u32[]{:S(2)}) collective-permute-start(bf16[1,2,8,24,3200]{4,3,2,1,0:T(8,128)(2,1)S(1)} %bitcast_dynamic-update-slice_fusion.13), channel_id=1, source_target_pairs={{0,8},{8,0},{1,9},{9,1},{2,10},{10,2},{3,11},{11,3},{4,12},{12,4},... | collective-permute-start | bytes 7372808 | tf_op jit(solution)/shard_map/ppermute | solution.py:215
  120.5 49.5 %collective-permute-start.9 = (bf16[1,2,8,24,3200]{4,3,2,1,0:T(8,128)(2,1)}, bf16[1,2,8,24,3200]{4,3,2,1,0:T(8,128)(2,1)}, u32[]{:S(2)}, u32[]{:S(2)}) collective-permute-start(bf16[1,2,8,24,3200]{4,3,2,1,0:T(8,128)(2,1)} %bitcast_dynamic-update-slice_fusion.6), channel_id=1, source_target_pairs={{0,8},{8,0},{1,9},{9,1},{2,10},{10,2},{3,11},{11,3},{4,12},{12,4},... | collective-permute-start | bytes 7372808 | tf_op jit(solution)/shard_map/ppermute | solution.py:215
  135.1 5.2 %copy-start.18 = (bf16[1,128,768]{2,1,0:T(8,128)(2,1)S(1)}, bf16[1,128,768]{2,1,0:T(8,128)(2,1)}, u32[]{:S(2)}) copy-start(bf16[1,128,768]{2,1,0:T(8,128)(2,1)} %get-tuple-element.88) | copy-start | bytes 589828
  136.2 30.5 %collective-permute-start = (bf16[432,768]{1,0:T(8,128)(2,1)}, bf16[432,768]{1,0:T(8,128)(2,1)}, u32[]{:S(2)}, u32[]{:S(2)}) collective-permute-start(bf16[432,768]{1,0:T(8,128)(2,1)} %pad_maximum_fusion.5), channel_id=1, source_target_pairs={{0,16},{16,0},{1,17},{17,1},{2,18},{18,2},{3,19},{19,3},{4,20},{20... | collective-permute-start | bytes 1990664 | tf_op jit(solution)/shard_map/ppermute | solution.py:215
  138.0 28.4 %collective-permute-start.22 = (bf16[3,128,768]{2,1,0:T(8,128)(2,1)}, bf16[3,128,768]{2,1,0:T(8,128)(2,1)S(1)}, u32[]{:S(2)}, u32[]{:S(2)}) collective-permute-start(bf16[3,128,768]{2,1,0:T(8,128)(2,1)} %maximum_select_fusion.1), channel_id=1, source_target_pairs={{0,16},{16,0},{1,17},{17,1},{2,18},{18,2},{3,19},{19,3},{4,20},{20... | collective-permute-start | bytes 1769480 | tf_op jit(solution)/shard_map/ppermute | solution.py:215
  170.0 39.9 %collective-permute-start.20 = (bf16[1,2,768,768]{3,2,1,0:T(8,128)(2,1)}, bf16[1,2,768,768]{3,2,1,0:T(8,128)(2,1)}, u32[]{:S(2)}, u32[]{:S(2)}) collective-permute-start(bf16[1,2,768,768]{3,2,1,0:T(8,128)(2,1)} %bitcast.372), channel_id=1, source_target_pairs={{0,8},{8,0},{1,9},{9,1},{2,10},{10,2},{3,11},{11,3},{4,12},{12,4},... | collective-permute-start | bytes 7077896 | tf_op jit(solution)/shard_map/ppermute | solution.py:215
  186.1 9.2 %copy-start.3 = (bf16[3,128,768]{2,1,0:T(8,128)(2,1)S(1)}, bf16[3,128,768]{2,1,0:T(8,128)(2,1)}, u32[]{:S(2)}) copy-start(bf16[3,128,768]{2,1,0:T(8,128)(2,1)} %get-tuple-element.50) | copy-start | bytes 1769476
  199.6 10.3 %copy-start.12 = (bf16[2,768,768]{2,1,0:T(8,128)(2,1)S(1)}, bf16[2,768,768]{2,1,0:T(8,128)(2,1)}, u32[]{:S(2)}) copy-start(bf16[2,768,768]{2,1,0:T(8,128)(2,1)} %all-gather.2.cloned.1.call-done) | copy-start | bytes 7077892
  224.9 9.3 %copy-start.11 = (f32[768,768]{1,0:T(8,128)S(1)}, f32[768,768]{1,0:T(8,128)}, u32[]{:S(2)}) copy-start(f32[768,768]{1,0:T(8,128)} %get-tuple-element.48) | copy-start | bytes 7077892
  234.2 9.1 %copy-start.32 = (bf16[768,3072]{1,0:T(8,128)(2,1)S(1)}, bf16[768,3072]{1,0:T(8,128)(2,1)}, u32[]{:S(2)}) copy-start(bf16[768,3072]{1,0:T(8,128)(2,1)} %get-tuple-element.146) | copy-start | bytes 14155780
  263.3 72.2 %collective-permute-start.21 = (bf16[3,128,768]{2,1,0:T(8,128)(2,1)}, bf16[3,128,768]{2,1,0:T(8,128)(2,1)}, u32[]{:S(2)}, u32[]{:S(2)}) collective-permute-start(bf16[3,128,768]{2,1,0:T(8,128)(2,1)} %bitcast.79), channel_id=1, source_target_pairs={{0,16},{16,0},{1,17},{17,1},{2,18},{18,2},{3,19},{19,3},{4,20},{20... | collective-permute-start | bytes 1769480 | tf_op jit(solution)/shard_map/ppermute | solution.py:215
  283.5 4.6 %copy-start.2 = (bf16[768,2304]{1,0:T(8,128)(2,1)S(1)}, bf16[768,2304]{1,0:T(8,128)(2,1)}, u32[]{:S(2)}) copy-start(bf16[768,2304]{1,0:T(8,128)(2,1)} %attention_backward.1) | copy-start | bytes 10616836
  283.5 4.7 %copy-start.22 = (bf16[3,128,768]{2,1,0:T(8,128)(2,1)S(1)}, bf16[3,128,768]{2,1,0:T(8,128)(2,1)}, u32[]{:S(2)}) copy-start(bf16[3,128,768]{2,1,0:T(8,128)(2,1)} %pad_maximum_fusion.6) | copy-start | bytes 1769476
  283.5 4.9 %copy-start.24 = (bf16[384,768]{1,0:T(8,128)(2,1)S(1)}, bf16[384,768]{1,0:T(8,128)(2,1)}, u32[]{:S(2)}) copy-start(bf16[384,768]{1,0:T(8,128)(2,1)} %slice.257) | copy-start | bytes 1769476
  287.1 56.5 %collective-permute-start.33 = (bf16[1,2,8,24,3200]{4,3,1,2,0:T(8,128)(2,1)}, bf16[1,2,8,24,3200]{4,3,1,2,0:T(8,128)(2,1)}, u32[]{:S(2)}, u32[]{:S(2)}) collective-permute-start(bf16[1,2,8,24,3200]{4,3,1,2,0:T(8,128)(2,1)} %copy_bitcast_fusion), channel_id=1, source_target_pairs={{0,8},{8,0},{1,9},{9,1},{2,10},{10,2},{3,11},{11,3},{4,12},{12,4},... | collective-permute-start | bytes 7372808 | tf_op jit(solution)/shard_map/ppermute | solution.py:215
  299.2 6.0 %copy-start.15 = (bf16[768,768]{1,0:T(8,128)(2,1)S(1)}, bf16[768,768]{1,0:T(8,128)(2,1)}, u32[]{:S(2)}) copy-start(bf16[768,768]{1,0:T(8,128)(2,1)} %convolution_convert_fusion.3) | copy-start | bytes 3538948
  303.4 6.8 %slice-start = ((s8[4915200]{0:T(1024)(128)(4,1)}), s8[720896]{0:T(1024)(128)(4,1)S(1)}, s32[]{:S(2)}) async-start(s8[4915200]{0:T(1024)(128)(4,1)} %bitcast.366), calls=%async_computation.3 | async-start | bytes 1441792
  305.0 5.3 %slice-start.1 = ((s8[4915200]{0:T(1024)(128)(4,1)}), s8[4194304]{0:T(1024)(128)(4,1)S(1)}, s32[]{:S(2)}) async-start(s8[4915200]{0:T(1024)(128)(4,1)} %bitcast.366), calls=%async_computation.4 | async-start | bytes 8388608
  305.0 33.8 %collective-permute-start.42 = (bf16[1,2,8,96,768]{4,3,1,2,0:T(8,128)(2,1)}, bf16[1,2,8,96,768]{4,3,1,2,0:T(8,128)(2,1)}, u32[]{:S(2)}, u32[]{:S(2)}) collective-permute-start(bf16[1,2,8,96,768]{4,3,1,2,0:T(8,128)(2,1)} %bitcast.345), channel_id=1, source_target_pairs={{0,8},{8,0},{1,9},{9,1},{2,10},{10,2},{3,11},{11,3},{4,12},{12,4},... | collective-permute-start | bytes 7077896 | tf_op jit(solution)/shard_map/ppermute | solution.py:215
  310.0 35.3 %collective-permute-start.24 = (bf16[1,2,8,24,3200]{4,3,1,2,0:T(8,128)(2,1)}, bf16[1,2,8,24,3200]{4,3,1,2,0:T(8,128)(2,1)}, u32[]{:S(2)}, u32[]{:S(2)}) collective-permute-start(bf16[1,2,8,24,3200]{4,3,1,2,0:T(8,128)(2,1)} %copy_bitcast_fusion.1), channel_id=1, source_target_pairs={{0,8},{8,0},{1,9},{9,1},{2,10},{10,2},{3,11},{11,3},{4,12},{12,4},... | collective-permute-start | bytes 7372808 | tf_op jit(solution)/shard_map/ppermute | solution.py:215
  313.6 13.5 %copy-start.28 = (s32[4,1]{0,1:T(1,128)S(1)}, s32[4,1]{0,1:T(1,128)}, u32[]{:S(2)}) copy-start(s32[4,1]{0,1:T(1,128)} %param.23) | copy-start | bytes 52
  313.6 21.9 %copy-start.8 = (bf16[384,768]{1,0:T(8,128)(2,1)S(1)}, bf16[384,768]{1,0:T(8,128)(2,1)}, u32[]{:S(2)}) copy-start(bf16[384,768]{1,0:T(8,128)(2,1)} %get-tuple-element.76) | copy-start | bytes 1769476
  313.7 24.1 %collective-permute-start.23 = (bf16[3,128,768]{2,1,0:T(8,128)(2,1)S(1)}, bf16[3,128,768]{2,1,0:T(8,128)(2,1)S(1)}, u32[]{:S(2)}, u32[]{:S(2)}) collective-permute-start(bf16[3,128,768]{2,1,0:T(8,128)(2,1)S(1)} %bitcast.378), channel_id=1, source_target_pairs={{0,16},{16,0},{1,17},{17,1},{2,18},{18,2},{3,19},{19,3},{4,20},{20... | collective-permute-start | bytes 1769480 | tf_op jit(solution)/shard_map/ppermute | solution.py:215
  344.7 7.1 %collective-permute-start.34 = (bf16[1,2,24,3200]{3,2,1,0:T(8,128)(2,1)S(1)}, bf16[1,2,24,3200]{3,2,1,0:T(8,128)(2,1)S(1)}, u32[]{:S(2)}, u32[]{:S(2)}) collective-permute-start(bf16[1,2,24,3200]{3,2,1,0:T(8,128)(2,1)S(1)} %fusion.39), channel_id=1, source_target_pairs={{1,3},{3,5},{5,7},{7,6},{6,4},{4,2},{2,0},{0,1},{9,8},{11,9},{13,1... | collective-permute-start | bytes 921608 | tf_op jit(solution)/shard_map/ppermute | solution.py:211
  346.5 12.3 %collective-permute-start.25 = (bf16[1,2,24,3200]{3,2,1,0:T(8,128)(2,1)S(1)}, bf16[1,2,24,3200]{3,2,1,0:T(8,128)(2,1)S(1)}, u32[]{:S(2)}, u32[]{:S(2)}) collective-permute-start(bf16[1,2,24,3200]{3,2,1,0:T(8,128)(2,1)S(1)} %fusion.53), channel_id=1, source_target_pairs={{1,3},{3,5},{5,7},{7,6},{6,4},{4,2},{2,0},{0,1},{9,8},{11,9},{13,1... | collective-permute-start | bytes 921608 | tf_op jit(solution)/shard_map/ppermute | solution.py:211
  353.0 15.4 %collective-permute-start.35 = (bf16[1,2,24,3200]{3,2,1,0:T(8,128)(2,1)S(1)}, bf16[1,2,24,3200]{3,2,1,0:T(8,128)(2,1)S(1)}, u32[]{:S(2)}, u32[]{:S(2)}) collective-permute-start(bf16[1,2,24,3200]{3,2,1,0:T(8,128)(2,1)S(1)} %fusion.38), channel_id=1, source_target_pairs={{1,3},{3,5},{5,7},{7,6},{6,4},{4,2},{2,0},{0,1},{9,8},{11,9},{13,1... | collective-permute-start | bytes 921608 | tf_op jit(solution)/shard_map/ppermute | solution.py:211
  360.0 18.9 %collective-permute-start.26 = (bf16[1,2,24,3200]{3,2,1,0:T(8,128)(2,1)S(1)}, bf16[1,2,24,3200]{3,2,1,0:T(8,128)(2,1)S(1)}, u32[]{:S(2)}, u32[]{:S(2)}) collective-permute-start(bf16[1,2,24,3200]{3,2,1,0:T(8,128)(2,1)S(1)} %fusion.52), channel_id=1, source_target_pairs={{1,3},{3,5},{5,7},{7,6},{6,4},{4,2},{2,0},{0,1},{9,8},{11,9},{13,1... | collective-permute-start | bytes 921608 | tf_op jit(solution)/shard_map/ppermute | solution.py:211
  369.6 14.3 %collective-permute-start.36 = (bf16[1,2,24,3200]{3,2,1,0:T(8,128)(2,1)S(1)}, bf16[1,2,24,3200]{3,2,1,0:T(8,128)(2,1)S(1)}, u32[]{:S(2)}, u32[]{:S(2)}) collective-permute-start(bf16[1,2,24,3200]{3,2,1,0:T(8,128)(2,1)S(1)} %fusion.36), channel_id=1, source_target_pairs={{1,3},{3,5},{5,7},{7,6},{6,4},{4,2},{2,0},{0,1},{9,8},{11,9},{13,1... | collective-permute-start | bytes 921608 | tf_op jit(solution)/shard_map/ppermute | solution.py:211
  380.1 7.2 %collective-permute-start.27 = (bf16[1,2,24,3200]{3,2,1,0:T(8,128)(2,1)S(1)}, bf16[1,2,24,3200]{3,2,1,0:T(8,128)(2,1)S(1)}, u32[]{:S(2)}, u32[]{:S(2)}) collective-permute-start(bf16[1,2,24,3200]{3,2,1,0:T(8,128)(2,1)S(1)} %fusion.50), channel_id=1, source_target_pairs={{1,3},{3,5},{5,7},{7,6},{6,4},{4,2},{2,0},{0,1},{9,8},{11,9},{13,1... | collective-permute-start | bytes 921608 | tf_op jit(solution)/shard_map/ppermute | solution.py:211
  385.1 6.9 %collective-permute-start.37 = (bf16[1,2,24,3200]{3,2,1,0:T(8,128)(2,1)S(1)}, bf16[1,2,24,3200]{3,2,1,0:T(8,128)(2,1)S(1)}, u32[]{:S(2)}, u32[]{:S(2)}) collective-permute-start(bf16[1,2,24,3200]{3,2,1,0:T(8,128)(2,1)S(1)} %fusion.34), channel_id=1, source_target_pairs={{1,3},{3,5},{5,7},{7,6},{6,4},{4,2},{2,0},{0,1},{9,8},{11,9},{13,1... | collective-permute-start | bytes 921608 | tf_op jit(solution)/shard_map/ppermute | solution.py:211
  388.4 8.0 %collective-permute-start.28 = (bf16[1,2,24,3200]{3,2,1,0:T(8,128)(2,1)S(1)}, bf16[1,2,24,3200]{3,2,1,0:T(8,128)(2,1)S(1)}, u32[]{:S(2)}, u32[]{:S(2)}) collective-permute-start(bf16[1,2,24,3200]{3,2,1,0:T(8,128)(2,1)S(1)} %fusion.48), channel_id=1, source_target_pairs={{1,3},{3,5},{5,7},{7,6},{6,4},{4,2},{2,0},{0,1},{9,8},{11,9},{13,1... | collective-permute-start | bytes 921608 | tf_op jit(solution)/shard_map/ppermute | solution.py:211
  393.2 6.9 %collective-permute-start.38 = (bf16[1,2,24,3200]{3,2,1,0:T(8,128)(2,1)S(1)}, bf16[1,2,24,3200]{3,2,1,0:T(8,128)(2,1)S(1)}, u32[]{:S(2)}, u32[]{:S(2)}) collective-permute-start(bf16[1,2,24,3200]{3,2,1,0:T(8,128)(2,1)S(1)} %fusion.32), channel_id=1, source_target_pairs={{1,3},{3,5},{5,7},{7,6},{6,4},{4,2},{2,0},{0,1},{9,8},{11,9},{13,1... | collective-permute-start | bytes 921608 | tf_op jit(solution)/shard_map/ppermute | solution.py:211
  397.6 7.3 %collective-permute-start.29 = (bf16[1,2,24,3200]{3,2,1,0:T(8,128)(2,1)S(1)}, bf16[1,2,24,3200]{3,2,1,0:T(8,128)(2,1)S(1)}, u32[]{:S(2)}, u32[]{:S(2)}) collective-permute-start(bf16[1,2,24,3200]{3,2,1,0:T(8,128)(2,1)S(1)} %fusion.46), channel_id=1, source_target_pairs={{1,3},{3,5},{5,7},{7,6},{6,4},{4,2},{2,0},{0,1},{9,8},{11,9},{13,1... | collective-permute-start | bytes 921608 | tf_op jit(solution)/shard_map/ppermute | solution.py:211
  401.3 10.9 %collective-permute-start.39 = (bf16[1,2,24,3200]{3,2,1,0:T(8,128)(2,1)S(1)}, bf16[1,2,24,3200]{3,2,1,0:T(8,128)(2,1)S(1)}, u32[]{:S(2)}, u32[]{:S(2)}) collective-permute-start(bf16[1,2,24,3200]{3,2,1,0:T(8,128)(2,1)S(1)} %fusion.30), channel_id=1, source_target_pairs={{1,3},{3,5},{5,7},{7,6},{6,4},{4,2},{2,0},{0,1},{9,8},{11,9},{13,1... | collective-permute-start | bytes 921608 | tf_op jit(solution)/shard_map/ppermute | solution.py:211
  406.1 14.9 %collective-permute-start.30 = (bf16[1,2,24,3200]{3,2,1,0:T(8,128)(2,1)S(1)}, bf16[1,2,24,3200]{3,2,1,0:T(8,128)(2,1)S(1)}, u32[]{:S(2)}, u32[]{:S(2)}) collective-permute-start(bf16[1,2,24,3200]{3,2,1,0:T(8,128)(2,1)S(1)} %fusion.44), channel_id=1, source_target_pairs={{1,3},{3,5},{5,7},{7,6},{6,4},{4,2},{2,0},{0,1},{9,8},{11,9},{13,1... | collective-permute-start | bytes 921608 | tf_op jit(solution)/shard_map/ppermute | solution.py:211
  413.4 11.0 %collective-permute-start.40 = (bf16[1,2,24,3200]{3,2,1,0:T(8,128)(2,1)S(1)}, bf16[1,2,24,3200]{3,2,1,0:T(8,128)(2,1)S(1)}, u32[]{:S(2)}, u32[]{:S(2)}) collective-permute-start(bf16[1,2,24,3200]{3,2,1,0:T(8,128)(2,1)S(1)} %fusion.28), channel_id=1, source_target_pairs={{1,3},{3,5},{5,7},{7,6},{6,4},{4,2},{2,0},{0,1},{9,8},{11,9},{13,1... | collective-permute-start | bytes 921608 | tf_op jit(solution)/shard_map/ppermute | solution.py:211
  422.2 7.9 %collective-permute-start.31 = (bf16[1,2,24,3200]{3,2,1,0:T(8,128)(2,1)S(1)}, bf16[1,2,24,3200]{3,2,1,0:T(8,128)(2,1)S(1)}, u32[]{:S(2)}, u32[]{:S(2)}) collective-permute-start(bf16[1,2,24,3200]{3,2,1,0:T(8,128)(2,1)S(1)} %fusion.42), channel_id=1, source_target_pairs={{1,3},{3,5},{5,7},{7,6},{6,4},{4,2},{2,0},{0,1},{9,8},{11,9},{13,1... | collective-permute-start | bytes 921608 | tf_op jit(solution)/shard_map/ppermute | solution.py:211
  425.5 6.8 %collective-permute-start.41 = (bf16[24,3200]{1,0:T(8,128)(2,1)S(1)}, bf16[24,3200]{1,0:T(8,128)(2,1)S(1)}, u32[]{:S(2)}, u32[]{:S(2)}) collective-permute-start(bf16[24,3200]{1,0:T(8,128)(2,1)S(1)} %fusion.64), channel_id=1, source_target_pairs={{0,16},{16,0},{1,17},{17,1},{2,18},{18,2},{3,19},{19,3},{4,20},{20... | collective-permute-start | bytes 460808 | tf_op jit(solution)/shard_map/ppermute | solution.py:215
  431.3 6.5 %collective-permute-start.32 = (bf16[24,3200]{1,0:T(8,128)(2,1)S(1)}, bf16[24,3200]{1,0:T(8,128)(2,1)S(1)}, u32[]{:S(2)}, u32[]{:S(2)}) collective-permute-start(bf16[24,3200]{1,0:T(8,128)(2,1)S(1)} %fusion.63), channel_id=1, source_target_pairs={{0,16},{16,0},{1,17},{17,1},{2,18},{18,2},{3,19},{19,3},{4,20},{20... | collective-permute-start | bytes 460808 | tf_op jit(solution)/shard_map/ppermute | solution.py:215
  439.8 5.2 %collective-permute-start.43 = (bf16[96,768]{1,0:T(8,128)(2,1)S(1)}, bf16[96,768]{1,0:T(8,128)(2,1)S(1)}, u32[]{:S(2)}, u32[]{:S(2)}) collective-permute-start(bf16[96,768]{1,0:T(8,128)(2,1)S(1)} %get-tuple-element.101), channel_id=1, source_target_pairs={{0,16},{16,0},{1,17},{17,1},{2,18},{18,2},{3,19},{19,3},{4,20},{20... | collective-permute-start | bytes 442376 | tf_op jit(solution)/shard_map/ppermute | solution.py:215
  (17 other events, 49.4 us)
Sparse Core Ops, SparseCore 0:
  39.7 62.5 all-gather.1
  343.7 78.2 reduce-scatter.1
